TPU v7x, 32 devices: a whole 2x2x4 slice. The times are simulated.
32 devices in a mesh: grp: 2 (over y), tm: 16 (over z, x, core).
Axes of the slice: x: 2, y: 2, z: 4, core: 2. Of those that a mesh axis runs over, the one named last changes fastest.
Arguments:
- residual: bfloat16 [4, 2, 4096, 2048], P('grp', None, 'tm'), parts along dimension 0, may hold values from -6 to 6
- eigenbasis: bfloat16 [2048, 2048], P('tm'), may hold values from -0.125 to 0.125
- eigenvalues: float32 [2048], replicated, may hold values from 0.05 to 5
- node_order: int32 [2048], replicated, may hold values from 0 to 2047, each once
Outputs:
- correction: float32 [4, 2, 4096, 2048], P('grp', None, 'tm'), parts along dimension 0
There are 2 independent parts, one for each index of `grp`. A program takes and returns all parts, laid end to end along the dimension named above; an argument that names none is the same for every part. Nothing has to cross between parts.
Inputs may be any that keep to these rules, and one draw needn't show every extreme that they name: node_order names every number of 0 to 2047 exactly once.
All inputs are finite; a program needn't handle non-finite values.
Results may differ from a plain program's by a relative error of at most 0.0055.
Values may be sent and summed in bfloat16 or wider, within the bound.
A program may use at most 64 MiB of HBM per device.

v0:
```python
import functools

import jax
import jax.numpy as jnp
from jax import lax
from jax.experimental import pallas as pl
from jax.experimental.pallas import tpu as pltpu
from jax.sharding import PartitionSpec as P

SEGMENTS = 8


def mul(a, b):
    return a[0] * b[0] - a[1] * b[1], a[0] * b[1] + a[1] * b[0]


def add(a, b):
    return a[0] + b[0], a[1] + b[1]


def sub(a, b):
    return a[0] - b[0], a[1] - b[1]


def inverse_of(a):
    size = a[0] * a[0] + a[1] * a[1]
    return a[0] / size, -a[1] / size


def power(a, exponent):
    result, square = None, a
    while exponent:
        if exponent & 1:
            result = square if result is None else mul(result, square)
        exponent >>= 1
        if exponent:
            square = mul(square, square)
    return result


def decay_root(mu):
    wide = 2.0 + mu
    disc_re, disc_im = wide * wide - 5.0, -2.0 * wide
    size = jnp.sqrt(disc_re * disc_re + disc_im * disc_im)
    sqrt_re = jnp.sqrt(0.5 * (size + disc_re))
    sqrt_im = 0.5 * disc_im / sqrt_re
    half = inverse_of((wide + sqrt_re, sqrt_im - 1.0))
    return 2.0 * half[0], 2.0 * half[1]


def carries_kernel(modal_ref, mu_ref, perm_ref, zp_ref, seg_ref, dev_ref, z_ref):
    vectors, _, steps, width = modal_ref.shape
    per_seg = steps // SEGMENTS
    root = decay_root(mu_ref[...])
    root8 = tuple(jnp.broadcast_to(x, (SEGMENTS, width)) for x in root)
    jump = power(root, per_seg)
    for r in range(vectors):
        for f in range(2):
            rows = jnp.dot(perm_ref[...], modal_ref[r, f], preferred_element_type=jnp.float32)
            z_ref[r, f] = rows
            zp_ref[r, f] = rows.astype(jnp.bfloat16)
    for r in range(vectors):
        def at(k):
            here = pl.ds(k * SEGMENTS, SEGMENTS)
            return z_ref[r, 0, here, :], z_ref[r, 1, here, :]

        ahead, behind = at(0), at(per_seg - 1)
        for k in range(1, per_seg):
            ahead = add(at(k), mul(root8, ahead))
            behind = add(at(per_seg - 1 - k), mul(root8, behind))
        for c in range(2):
            seg_ref[r, 0, c] = ahead[c]
            seg_ref[r, 1, c] = behind[c]
        row = lambda a, s: (a[0][s:s + 1], a[1][s:s + 1])
        front, back = row(ahead, 0), row(behind, SEGMENTS - 1)
        for s in range(1, SEGMENTS):
            front = add(row(ahead, s), mul(jump, front))
            back = add(row(behind, SEGMENTS - 1 - s), mul(jump, back))
        for c in range(2):
            dev_ref[r, 0, c] = front[c]
            dev_ref[r, 1, c] = back[c]


def solve_kernel(zp_ref, seg_ref, edge_ref, mu_ref, perm_ref, out_ref, p_ref, u_ref):
    vectors, _, steps, width = zp_ref.shape
    per_seg = steps // SEGMENTS
    root = decay_root(mu_ref[...])
    root8 = tuple(jnp.broadcast_to(x, (SEGMENTS, width)) for x in root)
    jump = power(root, per_seg)
    square = mul(root, root)
    gain = mul(root, inverse_of((1.0 - square[0], -square[1])))
    for r in range(vectors):
        row = lambda a, s: (seg_ref[r, a, 0, s:s + 1, :], seg_ref[r, a, 1, s:s + 1, :])
        lefts = [(edge_ref[r, 0, 0], edge_ref[r, 0, 1])]
        rights = [(edge_ref[r, 1, 0], edge_ref[r, 1, 1])]
        for s in range(SEGMENTS):
            lefts.append(add(row(0, s), mul(jump, lefts[-1])))
        for s in range(SEGMENTS - 1, 0, -1):
            rights.append(add(row(1, s), mul(jump, rights[-1])))
        rights = rights[::-1]
        ends = [mul(gain, add(rights[s], mul(root, lefts[s + 1]))) for s in range(SEGMENTS)]
        stack = lambda rows: tuple(jnp.concatenate([x[c] for x in rows], axis=0) for c in range(2))
        p = stack(lefts[:SEGMENTS])
        for k in range(0, per_seg, 2):
            both = pl.ds(k * SEGMENTS, 2 * SEGMENTS)
            pair = [zp_ref[r, f, both, :].astype(jnp.float32) for f in range(2)]
            for h in range(2):
                z = tuple(x[h * SEGMENTS:(h + 1) * SEGMENTS] for x in pair)
                p = add(z, mul(root8, p))
                for c in range(2):
                    p_ref[c, pl.ds((k + h) * SEGMENTS, SEGMENTS), :] = p[c]
        u = stack(ends)
        for k in range(per_seg - 2, -1, -2):
            later = []
            for h in (1, 0):
                here = pl.ds((k + h) * SEGMENTS, SEGMENTS)
                u = mul(root8, add((p_ref[0, here, :], p_ref[1, here, :]), u))
                later.append(u)
            both = pl.ds(k * SEGMENTS, 2 * SEGMENTS)
            for c in range(2):
                u_ref[c, both, :] = jnp.concatenate([later[1][c], later[0][c]], axis=0).astype(jnp.bfloat16)
        for c in range(2):
            out_ref[r, c] = jnp.dot(perm_ref[...], u_ref[c], preferred_element_type=jnp.float32).astype(jnp.bfloat16)


def gather_kernel(chips, mine_ref, node_ref, out_ref, held, send_sem, recv_sem, pair_send, pair_recv):
    _, _, rows, modes = held.shape
    states = out_ref.shape[0]
    pieces = 4
    part = modes // pieces
    tile = min(512, states)
    me = lax.axis_index("tm")
    core, chip = me % 2, me // 2
    odd = chip % 2
    place = (1 - odd) * (chip // 2) + odd * (chips - 1 - chip // 2)

    def chip_at(position):
        position = (position + chips) % chips
        second = position // (chips // 2)
        return (1 - second) * 2 * position + second * (2 * (chips - 1 - position) + 1)

    targets = (chip_at(place + 1) * 2 + core, chip_at(place - 1) * 2 + core)
    pair = chip * 2 + 1 - core

    def piece(step, i):
        source = chip_at(place - step if i % 2 == 0 else place + step)
        return source, held.at[source, core, :, pl.ds(i * part, part)]

    def ring(step, i):
        _, ref = piece(step, i)
        return pltpu.make_async_remote_copy(
            src_ref=ref, dst_ref=ref, send_sem=send_sem.at[step, i], recv_sem=recv_sem.at[step, i],
            device_id={"tm": targets[i % 2]}, device_id_type=pl.DeviceIdType.MESH,
        )

    def landed(step, i):
        _, ref = piece(step + 1, i)
        return pltpu.make_async_remote_copy(
            src_ref=ref, dst_ref=ref, send_sem=send_sem.at[step, i], recv_sem=recv_sem.at[step, i],
            device_id={"tm": targets[i % 2]}, device_id_type=pl.DeviceIdType.MESH,
        )

    def share(step, i):
        _, ref = piece(step, i)
        return pltpu.make_async_remote_copy(
            src_ref=ref, dst_ref=ref, send_sem=pair_send.at[step, i], recv_sem=pair_recv.at[step, i],
            device_id={"tm": pair}, device_id_type=pl.DeviceIdType.MESH,
        )

    def place_rows(step, i, first):
        if i < 2:
            return
        source, _ = piece(step, i)
        nodes = node_ref[source]

        def one_tile(t, carry):
            start = pl.multiple_of(t * tile, tile)
            index = lax.broadcasted_iota(jnp.int32, (tile, 2 * rows), 0) + start
            choose = jnp.where(index == nodes, 1.0, 0.0).astype(jnp.bfloat16)
            here = pl.ds(start, tile)
            for c in (i - 2, i):
                columns = pl.ds(c * part, part)
                block = held[source, :, :, columns].reshape(2 * rows, part)
                moved = jnp.dot(choose, block, preferred_element_type=jnp.float32).astype(jnp.bfloat16)
                out_ref[here, columns] = moved if first else moved + out_ref[here, columns]
            return carry

        lax.fori_loop(0, states // tile, one_tile, 0)

    held[chip, core] = mine_ref[...]
    barrier = pltpu.get_barrier_semaphore()
    for target in (*targets, pair):
        pl.semaphore_signal(barrier, inc=1, device_id={"tm": target}, device_id_type=pl.DeviceIdType.MESH)
    pl.semaphore_wait(barrier, 3)

    def one_step(step, first, last):
        for i in range(pieces):
            landed(step - 1, i).wait_recv()
            if not last:
                ring(step, i).start()
            share(step, i).start()
            share(step - 1, i).wait_recv()
            place_rows(step - 1, i, first)

    for i in range(pieces):
        ring(0, i).start()
        share(0, i).start()
    one_step(1, True, False)

    def body(step, carry):
        one_step(step, False, False)
        return carry

    lax.fori_loop(2, chips - 1, body, 0)
    one_step(chips - 1, False, True)
    for i in range(pieces):
        share(chips - 1, i).wait_recv()
        place_rows(chips - 1, i, False)

    def drain(step, carry):
        for i in range(pieces):
            ring(step, i).wait_send()
            share(step, i).wait_send()
        return carry

    lax.fori_loop(0, chips - 1, drain, 0)
    for i in range(pieces):
        share(chips - 1, i).wait_send()


def on_device(residual, eigenbasis, eigenvalues, node_order):
    vectors, fields, steps, states = residual.shape
    modes = eigenbasis.shape[1]
    parts = lax.axis_size("tm")
    me = lax.axis_index("tm")
    per_seg = steps // SEGMENTS
    width = min(256, modes)
    blocks = modes // width

    chips = parts // 2
    rows = eigenbasis.shape[0]
    basis = pl.pallas_call(
        functools.partial(gather_kernel, chips),
        out_shape=jax.ShapeDtypeStruct((states, modes), jnp.bfloat16),
        in_specs=[pl.BlockSpec(memory_space=pltpu.VMEM)] * 2,
        out_specs=pl.BlockSpec(memory_space=pltpu.VMEM),
        scratch_shapes=[pltpu.VMEM((chips, 2, rows, modes), jnp.bfloat16)]
        + [pltpu.SemaphoreType.DMA((chips, 4))] * 4,
        compiler_params=pltpu.CompilerParams(
            collective_id=0, has_side_effects=True, vmem_limit_bytes=44 * 1024 * 1024
        ),
        name="gather_rows",
    )(eigenbasis, node_order.reshape(chips, 1, 2 * rows))

    modal = jnp.einsum("rfts,sj->rftj", residual, basis, preferred_element_type=jnp.float32).astype(jnp.bfloat16)

    row = jnp.arange(steps, dtype=jnp.int32)
    time_of_row = (row % SEGMENTS) * per_seg + row // SEGMENTS
    perm = (time_of_row[:, None] == row[None, :]).astype(jnp.bfloat16)
    mu = eigenvalues[None, :]

    f32 = jnp.float32
    wide_block = pl.BlockSpec((vectors, fields, steps, width), lambda j: (0, 0, 0, j))
    seg_block = pl.BlockSpec((vectors, 2, 2, SEGMENTS, width), lambda j: (0, 0, 0, 0, j))
    dev_block = pl.BlockSpec((vectors, 2, 2, 1, width), lambda j: (0, 0, 0, 0, j))
    mu_block = pl.BlockSpec((1, width), lambda j: (0, j))
    perm_block = pl.BlockSpec((steps, steps), lambda j: (0, 0))
    params = pltpu.CompilerParams(vmem_limit_bytes=40 * 1024 * 1024)
    zp, seg, dev = pl.pallas_call(
        carries_kernel,
        grid=(blocks,),
        in_specs=[wide_block, mu_block, perm_block],
        out_specs=[wide_block, seg_block, dev_block],
        out_shape=[
            jax.ShapeDtypeStruct((vectors, fields, steps, modes), jnp.bfloat16),
            jax.ShapeDtypeStruct((vectors, 2, 2, SEGMENTS, modes), f32),
            jax.ShapeDtypeStruct((vectors, 2, 2, 1, modes), f32),
        ],
        scratch_shapes=[pltpu.VMEM((vectors, fields, steps, width), f32)],
        compiler_params=params,
        name="carries",
    )(modal, mu, perm)

    root = decay_root(mu)
    hop = power(root, steps)
    one = (jnp.ones_like(mu), jnp.zeros_like(mu))
    zero = (jnp.zeros((vectors, modes), f32),) * 2
    pick = lambda keep, new, old: tuple(jnp.where(keep, a, b) for a, b in zip(new, old))
    group = dev[:, :, :, 0, :]
    left, right = zero, zero
    from_start, from_end, span, reach = one, one, hop, 1
    while reach < parts:
        other = lax.ppermute(group, "tm", [(d, d ^ reach) for d in range(parts)])
        upper = (me // reach) % 2 == 1
        low, high = jnp.where(upper, other, group), jnp.where(upper, group, other)
        low_front, high_front = (low[:, 0, 0], low[:, 0, 1]), (high[:, 0, 0], high[:, 0, 1])
        low_back, high_back = (low[:, 1, 0], low[:, 1, 1]), (high[:, 1, 0], high[:, 1, 1])
        left = pick(upper, add(left, mul(from_start, low_front)), left)
        right = pick(upper, right, add(right, mul(from_end, high_back)))
        from_start = pick(upper, mul(from_start, span), from_start)
        from_end = pick(upper, from_end, mul(from_end, span))
        front, back = add(high_front, mul(span, low_front)), add(low_back, mul(span, high_back))
        group = jnp.stack((jnp.stack(front, 1), jnp.stack(back, 1)), 1)
        span, reach = mul(span, span), 2 * reach
    all_left, all_right = (group[:, 0, 0], group[:, 0, 1]), (group[:, 1, 0], group[:, 1, 1])
    whole = mul(span, root)
    whole_sq = mul(whole, whole)
    scale = mul(root, inverse_of((1.0 - whole_sq[0], -whole_sq[1])))
    start_term = mul(scale, sub(all_right, mul(whole, all_left)))
    end_term = mul(scale, sub(all_left, mul(whole, all_right)))
    left = sub(left, mul(start_term, from_start))
    right = sub(right, mul(end_term, from_end))
    edge = jnp.stack((jnp.stack(left, 1), jnp.stack(right, 1)), 1)[:, :, :, None, :]

    back = pl.pallas_call(
        solve_kernel,
        grid=(blocks,),
        in_specs=[wide_block, seg_block, dev_block, mu_block, perm_block],
        out_specs=wide_block,
        out_shape=jax.ShapeDtypeStruct((vectors, fields, steps, modes), jnp.bfloat16),
        scratch_shapes=[
            pltpu.VMEM((2, steps, width), f32),
            pltpu.VMEM((2, steps, width), jnp.bfloat16),
        ],
        compiler_params=params,
        name="solve",
    )(zp, seg, edge, mu, perm.T)

    return jnp.einsum("rftj,sj->rfts", back, basis, preferred_element_type=jnp.float32)


def solution(mesh):
    placed = (P("grp", None, "tm", None), P("tm", None), P(), P())
    return jax.shard_map(
        on_device, mesh=mesh, in_specs=placed, out_specs=P("grp", None, "tm", None), check_vma=False
    )
```

profile of v0, /device:TPU:0, one launch (start us, length us, event | category | flops | bytes accessed | tf_op | source)
XLA Modules:
  0.0 112.6 jit_solution(9756642453571122671)
XLA Ops:
  0.0 0.1 fusion.7
  0.1 0.0 copy-start.3
  0.1 1.0 copy-done.3
  1.2 0.0 copy-start.5
  1.2 0.7 copy-done.5
  1.9 53.5 %gather_rows.1 = bf16[2048,2048]{1,0:T(8,128)(2,1)S(1)} custom-call(bf16[128,2048]{1,0:T(8,128)(2,1)S(1)} %copy-done.3, s32[8,1,256]{2,1,0:T(1,128)S(1)} %bitcast.363), custom_call_target="tpu_custom_call" | custom-call | tf_op jit(solution)/shard_map/gather_rows/pallas_call | solution.py:242
  55.4 0.0 copy-done.6
  55.4 0.0 copy-start
  55.4 0.0 copy-start.4
  55.4 9.2 %convert_bitcast_fusion.modal_ref = bf16[2,2,256,2048]{3,2,1,0:T(8,128)(2,1)S(1)} fusion(bf16[2,2,256,2048]{3,2,1,0:T(8,128)(2,1)S(1)} %copy-done.6, bf16[2048,2048]{1,0:T(8,128)(2,1)S(1)} %gather_rows.1), kind=kOutput, calls=%fused_computation.4 | convolution fusion | flops 8592031744 | bytes 16777216 | tf_op jit(solution)/shard_map/rfts,sj->rftj/dot_general | solution.py:255
  64.6 0.0 copy-done
  64.6 0.0 copy-done.4
  64.6 6.3 %carries.1 = (bf16[2,2,256,2048]{3,2,1,0:T(8,128)(2,1)S(1)}, f32[2,2,2,8,2048]{4,3,2,1,0:T(8,128)S(1)}, f32[2,2,2,1,2048]{4,3,2,1,0:T(1,128)S(1)}) custom-call(bf16[2,2,256,2048]{3,2,1,0:T(8,128)(2,1)S(1)} %convert_bitcast_fusion.modal_ref, f32[1,2048]{1,0:T(1,128)S(1)} %bitcast.361, bf16[256,256]{1,0:T(8,128)(2,1)S(1)} %get-tuple-element.62.perm_ref), custom_call_target="tpu_custom_call" | custom-call | tf_op jit(solution)/shard_map/carries/pallas_call | solution.py:269
  70.9 0.0 copy-start.1
  70.9 2.0 %copy-done.1 = bf16[2,2,256,2048]{3,2,1,0:T(8,128)(2,1)} copy-done((bf16[2,2,256,2048]{3,2,1,0:T(8,128)(2,1)}, bf16[2,2,256,2048]{3,2,1,0:T(8,128)(2,1)S(1)}, u32[]{:S(2)}) %copy-start.1) | copy-done | bytes 4194328
  72.9 0.1 copy.50
  73.0 0.1 collective-permute-start
  73.1 0.0 copy-start.2
  73.2 0.1 subtract_select_fusion.3
  73.2 1.1 collective-permute-done
  74.3 0.1 broadcast_select_fusion.4
  74.4 0.1 fusion.27
  74.5 0.1 maximum_bitcast_fusion
  74.6 0.1 copy.8
  74.7 1.4 %collective-permute-start.1 = (f32[2,2,2,2048]{3,1,2,0:T(2,128)S(1)}, f32[2,2,2,2048]{3,1,2,0:T(2,128)S(1)}, u32[]{:S(2)}, u32[]{:S(2)}) collective-permute-start(f32[2,2,2,2048]{3,1,2,0:T(2,128)S(1)} %copy.8), channel_id=1, source_target_pairs={{0,2},{1,3},{2,0},{3,1},{4,6},{5,7},{6,4},{7,5},{8,10},{9,11},{10,... | collective-permute-start | bytes 196616 | tf_op jit(solution)/shard_map/ppermute | solution.py:293
  76.1 2.9 %collective-permute-done.1 = f32[2,2,2,2048]{3,1,2,0:T(2,128)S(1)} collective-permute-done((f32[2,2,2,2048]{3,1,2,0:T(2,128)S(1)}, f32[2,2,2,2048]{3,1,2,0:T(2,128)S(1)}, u32[]{:S(2)}, u32[]{:S(2)}) %collective-permute-start.1) | collective-permute-done | bytes 65568 | tf_op jit(solution)/shard_map/ppermute | solution.py:293
  79.0 0.1 copy_select_fusion.2
  79.1 0.1 broadcast_select_fusion.2
  79.1 0.1 fusion.23
  79.4 0.1 copy.14
  79.4 0.8 collective-permute-start.2
  80.3 3.5 %collective-permute-done.2 = f32[2,2,2,2048]{3,1,2,0:T(2,128)S(1)} collective-permute-done((f32[2,2,2,2048]{3,1,2,0:T(2,128)S(1)}, f32[2,2,2,2048]{3,1,2,0:T(2,128)S(1)}, u32[]{:S(2)}, u32[]{:S(2)}) %collective-permute-start.2) | collective-permute-done | bytes 65568 | tf_op jit(solution)/shard_map/ppermute | solution.py:293
  83.8 0.1 copy_select_fusion.1
  83.9 0.1 broadcast_select_fusion.1
  83.9 0.1 fusion.19
  84.2 0.1 copy.20
  84.2 1.1 collective-permute-start.3
  85.3 4.8 %collective-permute-done.3 = f32[2,2,2,2048]{3,1,2,0:T(2,128)S(1)} collective-permute-done((f32[2,2,2,2048]{3,1,2,0:T(2,128)S(1)}, f32[2,2,2,2048]{3,1,2,0:T(2,128)S(1)}, u32[]{:S(2)}, u32[]{:S(2)}) %collective-permute-start.3) | collective-permute-done | bytes 65568 | tf_op jit(solution)/shard_map/ppermute | solution.py:293
  90.2 0.1 copy_select_fusion
  90.2 0.1 broadcast_select_fusion
  90.3 0.1 fusion.13
  90.5 0.2 fusion.10
  90.8 0.2 fusion.11
  91.0 0.2 fusion.9
  91.2 0.2 fusion.8
  91.5 0.0 copy-done.2
  91.5 7.8 %solve.1 = bf16[2,2,256,2048]{3,2,1,0:T(8,128)(2,1)S(1)} custom-call(bf16[2,2,256,2048]{3,2,1,0:T(8,128)(2,1)S(1)} %copy-done.2, f32[2,2,2,8,2048]{4,3,2,1,0:T(8,128)S(1)} %get-tuple-element.9.seg_ref, f32[2,2,2,1,2048]{4,3,2,1,0:T(1,128)S(1)} %broadcast_in_dim.13.edge_ref, f32[1,2048]{1,0:T(1,128)S(1)} %bitcast.362, ...), custom_call_target="tpu_custom_call" | custom-call | tf_op jit(solution)/shard_map/solve/pallas_call | solution.py:315
  99.3 13.3 %fusion = f32[2,2,256,2048]{3,2,1,0:T(8,128)} fusion(bf16[2,2,256,2048]{3,2,1,0:T(8,128)(2,1)S(1)} %solve.1, bf16[2048,2048]{1,0:T(8,128)(2,1)} %copy-done), kind=kOutput, calls=%fused_computation | convolution fusion | flops 8589934592 | bytes 20971520 | tf_op jit(solution)/shard_map/rftj,sj->rfts/dot_general | solution.py:329
  (19 shorter events, 0.5 us)
Async XLA Ops:
  0.1 1.0 copy-start.3
  1.2 0.7 copy-start.5
  1.9 53.5 %copy-start.6 = (bf16[2,2,256,2048]{3,2,1,0:T(8,128)(2,1)S(1)}, bf16[2,2,256,2048]{3,2,1,0:T(8,128)(2,1)}, u32[]{:S(2)}) copy-start(bf16[2,2,256,2048]{3,2,1,0:T(8,128)(2,1)} %param.4) | copy-start | bytes 12582916
  55.4 9.2 %copy-start = (bf16[2048,2048]{1,0:T(8,128)(2,1)}, bf16[2048,2048]{1,0:T(8,128)(2,1)S(1)}, u32[]{:S(2)}) copy-start(bf16[2048,2048]{1,0:T(8,128)(2,1)S(1)} %gather_rows.1) | copy-start | bytes 25165828
  55.4 9.2 %copy-start.4 = (f32[2048]{0:T(1024)S(1)}, f32[2048]{0:T(1024)}, u32[]{:S(2)}) copy-start(f32[2048]{0:T(1024)} %param.6) | copy-start | bytes 24580
  70.9 2.0 %copy-start.1 = (bf16[2,2,256,2048]{3,2,1,0:T(8,128)(2,1)}, bf16[2,2,256,2048]{3,2,1,0:T(8,128)(2,1)S(1)}, u32[]{:S(2)}) copy-start(bf16[2,2,256,2048]{3,2,1,0:T(8,128)(2,1)S(1)} %get-tuple-element.8.zp_ref) | copy-start | bytes 12582916
  73.0 1.3 %collective-permute-start = (f32[2,2,2,2048]{3,1,2,0:T(2,128)S(1)}, f32[2,2,2,2048]{3,1,2,0:T(2,128)S(1)}, u32[]{:S(2)}, u32[]{:S(2)}) collective-permute-start(f32[2,2,2,2048]{3,1,2,0:T(2,128)S(1)} %bitcast.364), channel_id=1, source_target_pairs={{0,1},{1,0},{2,3},{3,2},{4,5},{5,4},{6,7},{7,6},{8,9},{9,8},{10,11... | collective-permute-start | bytes 196616 | tf_op jit(solution)/shard_map/ppermute | solution.py:293
  73.1 18.4 %copy-start.2 = (bf16[2,2,256,2048]{3,2,1,0:T(8,128)(2,1)S(1)}, bf16[2,2,256,2048]{3,2,1,0:T(8,128)(2,1)}, u32[]{:S(2)}) copy-start(bf16[2,2,256,2048]{3,2,1,0:T(8,128)(2,1)} %copy-done.1) | copy-start | bytes 12582916
  74.7 4.3 %collective-permute-start.1 = (f32[2,2,2,2048]{3,1,2,0:T(2,128)S(1)}, f32[2,2,2,2048]{3,1,2,0:T(2,128)S(1)}, u32[]{:S(2)}, u32[]{:S(2)}) collective-permute-start(f32[2,2,2,2048]{3,1,2,0:T(2,128)S(1)} %copy.8), channel_id=1, source_target_pairs={{0,2},{1,3},{2,0},{3,1},{4,6},{5,7},{6,4},{7,5},{8,10},{9,11},{10,... | collective-permute-start | bytes 196616 | tf_op jit(solution)/shard_map/ppermute | solution.py:293
  79.4 4.3 %collective-permute-start.2 = (f32[2,2,2,2048]{3,1,2,0:T(2,128)S(1)}, f32[2,2,2,2048]{3,1,2,0:T(2,128)S(1)}, u32[]{:S(2)}, u32[]{:S(2)}) collective-permute-start(f32[2,2,2,2048]{3,1,2,0:T(2,128)S(1)} %copy.14), channel_id=1, source_target_pairs={{0,4},{1,5},{2,6},{3,7},{4,0},{5,1},{6,2},{7,3},{8,12},{9,13},{10,... | collective-permute-start | bytes 196616 | tf_op jit(solution)/shard_map/ppermute | solution.py:293
  84.2 5.9 %collective-permute-start.3 = (f32[2,2,2,2048]{3,1,2,0:T(2,128)S(1)}, f32[2,2,2,2048]{3,1,2,0:T(2,128)S(1)}, u32[]{:S(2)}, u32[]{:S(2)}) collective-permute-start(f32[2,2,2,2048]{3,1,2,0:T(2,128)S(1)} %copy.20), channel_id=1, source_target_pairs={{0,8},{1,9},{2,10},{3,11},{4,12},{5,13},{6,14},{7,15},{8,0},{9,1},... | collective-permute-start | bytes 196616 | tf_op jit(solution)/shard_map/ppermute | solution.py:293
where the time goes:
time: 113 us
  Pallas kernels  67.5 us (60%)
  matrix products  22.5 us (20%)
  waiting for transfers between devices  12.3 us (11%)
  local copies, waits for them, and re-layouts  4.04 us (4%)
  starting transfers between devices  3.41 us (3%)
  other arithmetic  2.43 us (2%)
    pallas_call x1, Pallas kernels, on_device(): pl.pallas_call(functools.partial(gather_kernel, chips), out_shape=jax.Sha...  53.5 us
    dot_general x1, matrix products, on_device(): jnp.einsum('rftj,sj->rfts', back, basis, preferred_element_type=jnp.float32)  13.3 us
    ppermute x4, waiting for transfers between devices, on_device(): other = lax.ppermute(group, 'tm', [(d, d ^ reach) for d in range(parts)])  12.3 us
    dot_general x1, matrix products, on_device(): jnp.einsum('rfts,sj->rftj', residual, basis, preferred_element_type=jnp.f...  9.21 us
    pallas_call x1, Pallas kernels, on_device(): pl.pallas_call(solve_kernel, grid=(blocks,), in_specs=[wide_block, seg_bl...  7.78 us
    pallas_call x1, Pallas kernels, on_device(): pl.pallas_call(carries_kernel, grid=(blocks,), in_specs=[wide_block, mu_b...  6.27 us
    unnamed x14, local copies, waits for them, and re-layouts  3.76 us
    ppermute x4, starting transfers between devices, on_device(): other = lax.ppermute(group, 'tm', [(d, d ^ reach) for d in range(parts)])  3.41 us
  transfers between devices with their start and end apart: 4, of which 4 were waited for; matrix products, arithmetic and copies ran while one was open for 0% of the time, Pallas kernels for 0%

commit v1 on v0

v1 whole, which is shorter than its diff:
```python
import functools

import jax
import jax.numpy as jnp
from jax import lax
from jax.experimental import pallas as pl
from jax.experimental.pallas import tpu as pltpu
from jax.sharding import PartitionSpec as P

SEGMENTS = 8
BLOCKS = 4
MESH = pl.DeviceIdType.MESH
F32, BF16 = jnp.float32, jnp.bfloat16


def mul(a, b):
    return a[0] * b[0] - a[1] * b[1], a[0] * b[1] + a[1] * b[0]


def add(a, b):
    return a[0] + b[0], a[1] + b[1]


def sub(a, b):
    return a[0] - b[0], a[1] - b[1]


def inverse_of(a):
    size = a[0] * a[0] + a[1] * a[1]
    return a[0] / size, -a[1] / size


def power(a, exponent):
    result, square = None, a
    while exponent:
        if exponent & 1:
            result = square if result is None else mul(result, square)
        exponent >>= 1
        if exponent:
            square = mul(square, square)
    return result


def decay_root(mu):
    wide = 2.0 + mu
    disc_re, disc_im = wide * wide - 5.0, -2.0 * wide
    size = jnp.sqrt(disc_re * disc_re + disc_im * disc_im)
    sqrt_re = jnp.sqrt(0.5 * (size + disc_re))
    sqrt_im = 0.5 * disc_im / sqrt_re
    half = inverse_of((wide + sqrt_re, sqrt_im - 1.0))
    return 2.0 * half[0], 2.0 * half[1]


def time_order(steps, transposed):
    per_seg = steps // SEGMENTS
    row = lax.broadcasted_iota(jnp.int32, (steps, steps), 1 if transposed else 0)
    col = lax.broadcasted_iota(jnp.int32, (steps, steps), 0 if transposed else 1)
    time = (row % SEGMENTS) * per_seg + row // SEGMENTS
    return jnp.where(time == col, 1.0, 0.0).astype(BF16)


def forward_kernel(
    chips, basis_ref, node_ref, mu_ref, unit_mu_ref, residual_ref,
    moved_out, z_out, seg_out, edge_out,
    held, choose, moved, rows_in, z, devs, devs_in, edges, edges_in,
    local_sem, pair_send, pair_recv, ring_send, ring_recv, y_send, y_recv,
    block_send, block_recv, dev_send, dev_recv, edge_send, edge_recv,
):
    vectors, fields, steps, states = residual_ref.shape
    rows, modes = basis_ref.shape
    width = moved.shape[3]
    piece = width // 2
    half_modes = modes // 2
    owners, lanes = devs.shape[0], devs.shape[3]
    parts = 2 * chips
    half = chips // 2
    per_seg = steps // SEGMENTS

    me, group = lax.axis_index("tm"), lax.axis_index("grp")
    core, chip = me % 2, me // 2
    other = 1 - core
    odd = chip % 2
    place = (1 - odd) * (chip // 2) + odd * (chips - 1 - chip // 2)

    def chip_at(position):
        position = (position + chips) % chips
        second = position // half
        return (1 - second) * 2 * position + second * (2 * (chips - 1 - position) + 1)

    targets = (chip_at(place + 1) * 2 + core, chip_at(place - 1) * 2 + core)
    pair = {"tm": chip * 2 + other}
    across = {"grp": 1 - group}
    order = (group, 1 - group, 2, 3)
    ring_blocks = (group, 2, 3)

    def load_rows(r, f):
        return pltpu.make_async_copy(residual_ref.at[r, f], rows_in.at[r, f], local_sem.at[8 + r * fields + f])

    def own_rows(b, i):
        columns = pl.ds(pl.multiple_of(core * half_modes + b * width + i * piece, piece), piece)
        return pltpu.make_async_copy(
            basis_ref.at[:, columns], held.at[b, i, chip, pl.ds(pl.multiple_of(core * rows, rows), rows)],
            local_sem.at[b * 2 + i],
        )

    def pair_rows(b, i, side, whose):
        columns = pl.ds(pl.multiple_of(side * half_modes + b * width + i * piece, piece), piece)
        return pltpu.make_async_remote_copy(
            src_ref=basis_ref.at[:, columns],
            dst_ref=held.at[b, i, chip, pl.ds(pl.multiple_of(whose * rows, rows), rows)],
            send_sem=pair_send.at[b * 2 + i], recv_sem=pair_recv.at[b * 2 + i],
            device_id=pair, device_id_type=MESH,
        )

    def ring(turn, s, d, i, behind):
        source = chip_at(place - (s - 1 + behind)) if d == 0 else chip_at(place + (s - 1 + behind))
        ref = held.at[ring_blocks[turn], i, source]
        at = (turn * 2 + d) * 2 + i
        return pltpu.make_async_remote_copy(
            src_ref=ref, dst_ref=ref, send_sem=ring_send.at[at, s - 1], recv_sem=ring_recv.at[at, s - 1],
            device_id={"tm": targets[d]}, device_id_type=MESH,
        )

    def over_y(i, source, b):
        ref = held.at[b, i, source]
        return pltpu.make_async_remote_copy(
            src_ref=ref, dst_ref=ref, send_sem=y_send.at[i, source], recv_sem=y_recv.at[i, source],
            device_id=across, device_id_type=MESH,
        )

    BOTH = ((0, 0), (0, 1), (1, 0), (1, 1))
    LAST = ((0, 0), (1, 1))

    def first_sends(turn):
        for d, i in (BOTH if half > 1 else LAST):
            ring(turn, 1, d, i, 0).start()

    def event(turn, s, kind):
        for d, i in (LAST if kind == "last" else BOTH):
            ring(turn, s, d, i, 1).wait_recv()
            if kind == "mid" or (kind == "next_last" and i == d):
                ring(turn, s + 1, d, i, 0).start()
            if turn == 0:
                source = chip_at(place - s) if d == 0 else chip_at(place + s)
                over_y(i, source, group).start()

    def phase(turn, p):
        if p == 0:
            if half - 3 == 1:
                event(turn, 1, "mid")
            elif half > 4:
                def body(s, carry):
                    event(turn, s, "mid")
                    return carry
                lax.fori_loop(1, half - 2, body, 0)
        elif half - 3 + p >= 1:
            event(turn, half - 3 + p, ("", "mid", "next_last", "last")[p])

    def build_choose(lo, hi):
        tile = min(256, states)

        def one(t, carry):
            start = pl.multiple_of(t * tile, tile)
            index = lax.broadcasted_iota(jnp.int32, (tile, states), 0) + start
            choose[pl.ds(start, tile), :] = jnp.where(index == node_ref[...], 1.0, 0.0).astype(BF16)
            return carry

        count = states // tile
        lax.fori_loop(lo * count // 4, hi * count // 4, one, 0)

    def order_rows(r):
        tile = min(512, states)
        perm = time_order(steps, False)
        for f in range(fields):
            load_rows(r, f).wait()

        def one(t, carry):
            here = pl.ds(pl.multiple_of(t * tile, tile), tile)
            for f in range(fields):
                rows_in[r, f, :, here] = jnp.dot(
                    perm, rows_in[r, f, :, here], preferred_element_type=F32
                ).astype(BF16)
            return carry

        lax.fori_loop(0, states // tile, one, 0)

    def permute(b):
        tile = min(512, states)

        def one(t, carry):
            here = pl.ds(pl.multiple_of(t * tile, tile), tile)
            moved[core, b, here, :] = jnp.dot(
                choose[here, :], jnp.concatenate([held[b, i].reshape(states, piece) for i in range(2)], axis=1),
                preferred_element_type=F32,
            ).astype(BF16)
            return carry

        lax.fori_loop(0, states // tile, one, 0)

    def hand_over(b, side):
        ref = moved.at[side, b]
        return pltpu.make_async_remote_copy(
            src_ref=ref, dst_ref=ref, send_sem=block_send.at[b], recv_sem=block_recv.at[b],
            device_id=pair, device_id_type=MESH,
        )

    def store_moved(h, b):
        return pltpu.make_async_copy(moved.at[h, b], moved_out.at[h, b], local_sem.at[8 + vectors * fields + h * BLOCKS + b])

    def store_z(h, b):
        return pltpu.make_async_copy(z.at[h, b], z_out.at[h, b], local_sem.at[8 + vectors * fields + (2 + h) * BLOCKS + b])

    def to_modes(h, b):
        root = decay_root(mu_ref[h, b])
        root8 = tuple(jnp.broadcast_to(x, (SEGMENTS, width)) for x in root)
        jump = power(root, per_seg)

        def one(r, carry):
            for f in range(fields):
                z[h, b, r, f] = jnp.dot(rows_in[r, f], moved[h, b], preferred_element_type=F32).astype(BF16)

            def pairs(k):
                both = pl.ds(k * SEGMENTS, 2 * SEGMENTS)
                full = [z[h, b, r, f, both, :].astype(F32) for f in range(2)]
                return [tuple(x[m * SEGMENTS:(m + 1) * SEGMENTS] for x in full) for m in range(2)]

            low, high = pairs(0), pairs(per_seg - 2)
            ahead = add(low[1], mul(root8, low[0]))
            behind = add(high[0], mul(root8, high[1]))
            for k in range(2, per_seg, 2):
                low, high = pairs(k), pairs(per_seg - 2 - k)
                ahead = add(low[0], mul(root8, ahead))
                ahead = add(low[1], mul(root8, ahead))
                behind = add(high[1], mul(root8, behind))
                behind = add(high[0], mul(root8, behind))
            for c in range(2):
                seg_out[h, b, r, 0, c] = ahead[c]
                seg_out[h, b, r, 1, c] = behind[c]
            row = lambda a, s: (a[0][s:s + 1], a[1][s:s + 1])
            front, back = row(ahead, 0), row(behind, SEGMENTS - 1)
            for s in range(1, SEGMENTS):
                front = add(row(ahead, s), mul(jump, front))
                back = add(row(behind, SEGMENTS - 1 - s), mul(jump, back))
            slab = (h * half_modes + b * width) // lanes
            for j in range(width // lanes):
                cut = slice(j * lanes, (j + 1) * lanes)
                for c in range(2):
                    devs[slab + j, r, c:c + 1, :] = front[c][:, cut]
                    devs[slab + j, r, 2 + c:3 + c, :] = back[c][:, cut]
            return carry

        lax.fori_loop(0, vectors, one, 0)
        store_z(h, b).start()

    def send_devs(e):
        return pltpu.make_async_remote_copy(
            src_ref=devs.at[e], dst_ref=devs_in.at[me], send_sem=dev_send.at[e], recv_sem=dev_recv.at[me],
            device_id={"tm": e}, device_id_type=MESH,
        )

    def devs_from(d):
        return pltpu.make_async_remote_copy(
            src_ref=devs.at[0], dst_ref=devs_in.at[d], send_sem=dev_send.at[0], recv_sem=dev_recv.at[d],
            device_id=pair, device_id_type=MESH,
        )

    def send_edges(d):
        return pltpu.make_async_remote_copy(
            src_ref=edges.at[d], dst_ref=edges_in.at[me], send_sem=edge_send.at[d], recv_sem=edge_recv.at[me],
            device_id={"tm": d}, device_id_type=MESH,
        )

    def edges_from(e):
        return pltpu.make_async_remote_copy(
            src_ref=edges.at[0], dst_ref=edges_in.at[e], send_sem=edge_send.at[0], recv_sem=edge_recv.at[e],
            device_id=pair, device_id_type=MESH,
        )

    def others(count, act):
        def body(k, carry):
            d = (me + k) % parts
            if count == parts:
                act(d)
            else:
                pl.when(d < count)(lambda: act(d))
            return carry

        lax.fori_loop(1, parts, body, 0)

    def if_owner(act):
        if owners == parts:
            act()
        else:
            pl.when(me < owners)(act)

    def couple():
        root = decay_root(unit_mu_ref[me])
        hop = power(root, steps)
        whole = mul(power(hop, parts), root)
        square = mul(whole, whole)
        scale = mul(root, inverse_of((1.0 - square[0], -square[1])))
        zero = jnp.zeros((1, lanes), F32)
        for r in range(vectors):
            row = lambda ref, d, c: (ref[d, r, c:c + 1, :], ref[d, r, c + 1:c + 2, :])

            def scan(k, carry):
                left, right = carry
                d = parts - 1 - k
                for c in range(2):
                    edges[k, r, c:c + 1, :] = left[c]
                    edges[d, r, 2 + c:3 + c, :] = right[c]
                return add(row(devs_in, k, 0), mul(hop, left)), add(row(devs_in, d, 2), mul(hop, right))

            all_left, all_right = lax.fori_loop(0, parts, scan, ((zero, zero), (zero, zero)))
            start_term = mul(scale, sub(all_right, mul(whole, all_left)))
            end_term = mul(scale, sub(all_left, mul(whole, all_right)))

            def correct(k, carry):
                start_term, end_term = carry
                d = parts - 1 - k
                left, right = sub(row(edges, k, 0), start_term), sub(row(edges, d, 2), end_term)
                for c in range(2):
                    edges[k, r, c:c + 1, :] = left[c]
                    edges[d, r, 2 + c:3 + c, :] = right[c]
                return mul(hop, start_term), mul(hop, end_term)

            lax.fori_loop(0, parts, correct, (start_term, end_term))

    for r in range(vectors):
        for f in range(fields):
            load_rows(r, f).start()
    for b in range(BLOCKS):
        for i in range(2):
            own_rows(b, i).start()

    barrier = pltpu.get_barrier_semaphore()

    def greet(k, carry):
        pl.semaphore_signal(barrier, inc=1, device_id={"tm": (me + k) % parts}, device_id_type=MESH)
        return carry

    lax.fori_loop(1, parts, greet, 0)
    pl.semaphore_signal(barrier, inc=1, device_id=across, device_id_type=MESH)
    pl.semaphore_wait(barrier, parts)

    for b in order:
        for i in range(2):
            pair_rows(b, i, other, core).start()
    for b in ring_blocks[:1]:
        for i in range(2):
            own_rows(b, i).wait()
            pair_rows(b, i, core, other).wait_recv()
    first_sends(0)
    build_choose(0, 2)
    for b in order[1:]:
        for i in range(2):
            own_rows(b, i).wait()
            pair_rows(b, i, core, other).wait_recv()
    phase(0, 0)
    first_sends(1)
    build_choose(2, 4)
    phase(0, 1)
    order_rows(0)
    phase(1, 0)
    for r in range(1, vectors):
        order_rows(r)
    phase(0, 2)
    first_sends(2)
    phase(1, 1)
    phase(0, 3)

    def own_half(b):
        hand_over(b, core).start()
        store_moved(core, b).start()
        to_modes(core, b)

    def pair_half(b):
        hand_over(b, other).wait_recv()
        store_moved(other, b).start()
        to_modes(other, b)

    permute(group)
    phase(1, 2)
    own_half(group)
    phase(2, 0)
    pair_half(group)
    phase(1, 3)

    def from_y(k, carry):
        source = chip_at(place + k)
        for i in range(2):
            over_y(i, source, 1 - group).wait_recv()
        return carry

    lax.fori_loop(1, chips, from_y, 0)
    permute(1 - group)
    phase(2, 1)
    own_half(1 - group)
    phase(2, 2)
    pair_half(1 - group)
    permute(2)
    phase(2, 3)
    permute(3)
    own_half(2)
    pair_half(2)
    own_half(3)
    pair_half(3)

    others(owners, lambda e: send_devs(e).start())

    def settle():
        devs_in[me] = devs[me]
        others(parts, lambda d: devs_from(d).wait_recv())
        couple()
        others(parts, lambda d: send_edges(d).start())
        edges_in[me] = edges[me]

    if_owner(settle)
    others(owners, lambda e: edges_from(e).wait_recv())
    edge_out[...] = edges_in[...]

    others(owners, lambda e: send_devs(e).wait_send())
    if_owner(lambda: others(parts, lambda d: send_edges(d).wait_send()))
    for b in order:
        for i in range(2):
            pair_rows(b, i, other, core).wait_send()
        hand_over(b, core).wait_send()
        for h in range(2):
            store_moved(h, b).wait()
            store_z(h, b).wait()
    for turn in range(3):
        def drain(s, carry):
            for d, i in BOTH:
                ring(turn, s, d, i, 0).wait_send()
            return carry

        lax.fori_loop(1, half, drain, 0)
        for d, i in LAST:
            ring(turn, half, d, i, 0).wait_send()

    def y_drain(k, carry):
        source = chip_at(place + k)
        for i in range(2):
            over_y(i, source, group).wait_send()
        return carry

    lax.fori_loop(1, chips, y_drain, 0)


def backward_kernel(z_ref, seg_ref, edge_ref, mu_ref, moved_ref, out_ref, p_ref, u_ref, back_ref):
    _, _, vectors, fields, steps, width = z_ref.shape
    states = out_ref.shape[3]
    per_seg = steps // SEGMENTS
    slabs, lanes = edge_ref.shape[2], edge_ref.shape[5]
    perm = time_order(steps, True)
    for h in range(2):
        root = decay_root(mu_ref[h, 0])
        root8 = tuple(jnp.broadcast_to(x, (SEGMENTS, width)) for x in root)
        jump = power(root, per_seg)
        square = mul(root, root)
        gain = mul(root, inverse_of((1.0 - square[0], -square[1])))

        def edge(r, c):
            return jnp.concatenate([edge_ref[h, 0, j, r, c:c + 1, :] for j in range(slabs)], axis=1)

        for r in range(vectors):
            row = lambda a, s: (seg_ref[h, 0, r, a, 0, s:s + 1, :], seg_ref[h, 0, r, a, 1, s:s + 1, :])
            lefts = [(edge(r, 0), edge(r, 1))]
            rights = [(edge(r, 2), edge(r, 3))]
            for s in range(SEGMENTS):
                lefts.append(add(row(0, s), mul(jump, lefts[-1])))
            for s in range(SEGMENTS - 1, 0, -1):
                rights.append(add(row(1, s), mul(jump, rights[-1])))
            rights = rights[::-1]
            ends = [mul(gain, add(rights[s], mul(root, lefts[s + 1]))) for s in range(SEGMENTS)]
            stack = lambda rows: tuple(jnp.concatenate([x[c] for x in rows], axis=0) for c in range(2))
            p = stack(lefts[:SEGMENTS])
            for k in range(0, per_seg, 2):
                both = pl.ds(k * SEGMENTS, 2 * SEGMENTS)
                pair = [z_ref[h, 0, r, f, both, :].astype(F32) for f in range(2)]
                for m in range(2):
                    here = tuple(x[m * SEGMENTS:(m + 1) * SEGMENTS] for x in pair)
                    p = add(here, mul(root8, p))
                    for c in range(2):
                        p_ref[c, pl.ds((k + m) * SEGMENTS, SEGMENTS), :] = p[c]
            u = stack(ends)
            for k in range(per_seg - 2, -1, -2):
                later = []
                for m in (1, 0):
                    here = pl.ds((k + m) * SEGMENTS, SEGMENTS)
                    u = mul(root8, add((p_ref[0, here, :], p_ref[1, here, :]), u))
                    later.append(u)
                both = pl.ds(k * SEGMENTS, 2 * SEGMENTS)
                for c in range(2):
                    u_ref[c, both, :] = jnp.concatenate([later[1][c], later[0][c]], axis=0).astype(BF16)
            for c in range(2):
                back_ref[r, c, :, h * width:(h + 1) * width] = jnp.dot(
                    perm, u_ref[c], preferred_element_type=F32
                ).astype(BF16)

    tile = min(256, states)
    step = pl.program_id(0)

    def accumulate(first):
        def one(t, carry):
            here = pl.ds(pl.multiple_of(t * tile, tile), tile)
            block = jnp.concatenate([moved_ref[h, 0, here, :] for h in range(2)], axis=1)
            for r in range(vectors):
                for f in range(fields):
                    part = lax.dot_general(
                        back_ref[r, f], block, (((1,), (1,)), ((), ())), preferred_element_type=F32
                    )
                    out_ref[r, f, :, here] = part if first else out_ref[r, f, :, here] + part
            return carry

        lax.fori_loop(0, states // tile, one, 0)

    pl.when(step == 0)(lambda: accumulate(True))
    pl.when(step > 0)(lambda: accumulate(False))


def on_device(residual, eigenbasis, eigenvalues, node_order):
    vectors, fields, steps, states = residual.shape
    rows, modes = eigenbasis.shape
    parts = lax.axis_size("tm")
    chips = parts // 2
    width = modes // (2 * BLOCKS)
    owners = min(parts, modes // 128)
    lanes = modes // owners
    slabs = width // lanes
    vm, anyspace = pl.BlockSpec(memory_space=pltpu.VMEM), pl.BlockSpec(memory_space=pl.ANY)
    dma = pltpu.SemaphoreType.DMA
    mu = eigenvalues.reshape(2, BLOCKS, 1, width)
    moved, z, seg, edge = pl.pallas_call(
        functools.partial(forward_kernel, chips),
        out_shape=[
            jax.ShapeDtypeStruct((2, BLOCKS, states, width), BF16),
            jax.ShapeDtypeStruct((2, BLOCKS, vectors, fields, steps, width), BF16),
            jax.ShapeDtypeStruct((2, BLOCKS, vectors, 2, 2, SEGMENTS, width), F32),
            jax.ShapeDtypeStruct((owners, vectors, 4, lanes), F32),
        ],
        in_specs=[anyspace, vm, vm, vm, anyspace],
        out_specs=[anyspace, anyspace, vm, vm],
        scratch_shapes=[
            pltpu.VMEM((BLOCKS, 2, chips, 2 * rows, width // 2), BF16),
            pltpu.VMEM((states, states), BF16),
            pltpu.VMEM((2, BLOCKS, states, width), BF16),
            pltpu.VMEM((vectors, fields, steps, states), BF16),
            pltpu.VMEM((2, BLOCKS, vectors, fields, steps, width), BF16),
            pltpu.VMEM((owners, vectors, 4, lanes), F32),
            pltpu.VMEM((parts, vectors, 4, lanes), F32),
            pltpu.VMEM((parts, vectors, 4, lanes), F32),
            pltpu.VMEM((owners, vectors, 4, lanes), F32),
            dma((8 + vectors * fields + 4 * BLOCKS,)),
            dma((8,)), dma((8,)),
            dma((12, chips // 2)), dma((12, chips // 2)),
            dma((2, chips)), dma((2, chips)),
            dma((BLOCKS,)), dma((BLOCKS,)),
            dma((owners,)), dma((parts,)), dma((parts,)), dma((owners,)),
        ],
        compiler_params=pltpu.CompilerParams(
            collective_id=0, has_side_effects=True, vmem_limit_bytes=50 * 1024 * 1024
        ),
        name="forward",
    )(eigenbasis, node_order.reshape(1, states), mu, eigenvalues.reshape(owners, 1, lanes), residual)

    return pl.pallas_call(
        backward_kernel,
        grid=(BLOCKS,),
        in_specs=[
            pl.BlockSpec((2, 1, vectors, fields, steps, width), lambda b: (0, b, 0, 0, 0, 0)),
            pl.BlockSpec((2, 1, vectors, 2, 2, SEGMENTS, width), lambda b: (0, b, 0, 0, 0, 0, 0)),
            pl.BlockSpec((2, 1, slabs, vectors, 4, lanes), lambda b: (0, b, 0, 0, 0, 0)),
            pl.BlockSpec((2, 1, 1, width), lambda b: (0, b, 0, 0)),
            pl.BlockSpec((2, 1, states, width), lambda b: (0, b, 0, 0)),
        ],
        out_specs=pl.BlockSpec((vectors, fields, steps, states), lambda b: (0, 0, 0, 0)),
        out_shape=jax.ShapeDtypeStruct((vectors, fields, steps, states), F32),
        scratch_shapes=[
            pltpu.VMEM((2, steps, width), F32),
            pltpu.VMEM((2, steps, width), BF16),
            pltpu.VMEM((vectors, fields, steps, 2 * width), BF16),
        ],
        compiler_params=pltpu.CompilerParams(vmem_limit_bytes=50 * 1024 * 1024),
        name="backward",
    )(z, seg, edge.reshape(2, BLOCKS, slabs, vectors, 4, lanes), mu, moved)


def solution(mesh):
    placed = (P("grp", None, "tm", None), P("tm", None), P(), P())
    return jax.shard_map(
        on_device, mesh=mesh, in_specs=placed, out_specs=P("grp", None, "tm", None), check_vma=False
    )
```

time: 113 us -> 102 us (0.903)
  Pallas kernels: 67.5 us -> 98.4 us
  matrix products: 22.5 us -> 0 us
  waiting for transfers between devices: 12.3 us -> 0 us
  starting transfers between devices: 3.41 us -> 0 us
  other arithmetic: 2.43 us -> 0 us
    pallas_call x3 -> x2, Pallas kernels: 67.5 us -> 98.4 us  [the longest x1 72 us: on_device(): pl.pallas_call(functools.partial(forward_kernel, chips), out_shape=[jax.S...]
    dot_general x2 -> x0, matrix products: 22.5 us -> none  [the longest x1 13.3 us: on_device(): jnp.einsum('rftj,sj->rfts', back, basis, preferred_element_type=jnp.float32)]
    ppermute x4 -> x0, waiting for transfers between devices: 12.3 us -> none  [on_device(): other = lax.ppermute(group, 'tm', [(d, d ^ reach) for d in range(parts)])]
    ppermute x4 -> x0, starting transfers between devices: 3.41 us -> none  [on_device(): other = lax.ppermute(group, 'tm', [(d, d ^ reach) for d in range(parts)])]
    unnamed x14 -> x8, local copies, waits for them, and re-layouts: 3.76 us -> 3.13 us
  transfers between devices with their start and end apart: 4 -> 0, of which waited for: 4 -> 0; matrix products, arithmetic and copies ran while one was open for 0% -> 0% of each run, Pallas kernels for 0% -> 0%
where the time goes in v1:
time: 102 us
  Pallas kernels  98.4 us (96%)
  local copies, waits for them, and re-layouts  3.13 us (3%)
    pallas_call x1, Pallas kernels, on_device(): pl.pallas_call(functools.partial(forward_kernel, chips), out_shape=[jax.S...  72 us
    pallas_call x1, Pallas kernels, on_device(): pl.pallas_call(backward_kernel, grid=(BLOCKS,), in_specs=[pl.BlockSpec((2...  26.4 us
    unnamed x8, local copies, waits for them, and re-layouts  3.13 us

profile of v1, /device:TPU:0, one launch (start us, length us, event | category | flops | bytes accessed | tf_op | source)
XLA Modules:
  0.0 101.5 jit_solution(15752132160692712876)
XLA Ops:
  0.0 0.0 copy-start
  0.0 1.0 %copy-done = bf16[128,2048]{1,0:T(8,128)(2,1)S(1)} copy-done((bf16[128,2048]{1,0:T(8,128)(2,1)S(1)}, bf16[128,2048]{1,0:T(8,128)(2,1)}, u32[]{:S(2)}) %copy-start) | copy-done | bytes 524312
  1.0 0.0 copy-start.1
  1.0 0.7 copy-done.1
  1.7 0.0 copy-start.3
  1.7 0.7 copy-done.3
  2.4 72.0 %forward.1 = (bf16[2,4,2048,256]{3,2,1,0:T(8,128)(2,1)}, bf16[2,4,2,2,256,256]{5,4,3,2,1,0:T(8,128)(2,1)}, f32[2,4,2,2,2,8,256]{6,5,4,3,2,1,0:T(8,128)S(1)}, f32[16,2,4,128]{3,2,1,0:T(4,128)S(1)}) custom-call(bf16[128,2048]{1,0:T(8,128)(2,1)S(1)} %copy-done, s32[1,2048]{1,0:T(1,128)S(1)} %bitcast.8, f32[2,4,1,256]{3,2,1,0:T(1,128)S(1)} %bitcast.4, ...), custom_call_target="tpu_custom_call" | custom-call | tf_op jit(solution)/shard_map/forward/pallas_call | solution.py:534
  74.5 0.0 copy-start.2
  74.5 0.7 copy-done.2
  75.2 26.4 %backward.1 = f32[2,2,256,2048]{3,2,1,0:T(8,128)} custom-call(bf16[2,4,2,2,256,256]{5,4,3,2,1,0:T(8,128)(2,1)} %get-tuple-element.9.z_ref, f32[2,4,2,2,2,8,256]{6,5,4,3,2,1,0:T(8,128)S(1)} %get-tuple-element.10.seg_ref, f32[2,4,2,2,4,128]{5,4,3,2,1,0:T(4,128)S(1)} %bitcast.7, f32[2,4,1,256]{3,2,1,0:T(1,128)S(1)} %bitcast.6, ...), custom_call_target="tpu_custom_call" | custom-call | tf_op jit(solution)/shard_map/backward/pallas_call | solution.py:567
Async XLA Ops:
  0.0 1.0 %copy-start = (bf16[128,2048]{1,0:T(8,128)(2,1)S(1)}, bf16[128,2048]{1,0:T(8,128)(2,1)}, u32[]{:S(2)}) copy-start(bf16[128,2048]{1,0:T(8,128)(2,1)} %basis_ref.1) | copy-start | bytes 1572868
  1.0 0.7 copy-start.1
  1.7 0.7 copy-start.3
  74.5 0.7 copy-start.2

commit v2 on v1

--- a/solution.py
+++ b/solution.py
@@ -9,6 +9,7 @@
 
 SEGMENTS = 8
 BLOCKS = 4
+VMEM_BYTES = 62 * 1024 * 1024
 MESH = pl.DeviceIdType.MESH
 F32, BF16 = jnp.float32, jnp.bfloat16
 
@@ -93,8 +94,11 @@
     order = (group, 1 - group, 2, 3)
     ring_blocks = (group, 2, 3)
 
+    def part(r, f):
+        return pl.ds(pl.multiple_of((r * fields + f) * steps, steps), steps)
+
     def load_rows(r, f):
-        return pltpu.make_async_copy(residual_ref.at[r, f], rows_in.at[r, f], local_sem.at[8 + r * fields + f])
+        return pltpu.make_async_copy(residual_ref.at[r, f], rows_in.at[part(r, f)], local_sem.at[8 + r * fields + f])
 
     def own_rows(b, i):
         columns = pl.ds(pl.multiple_of(core * half_modes + b * width + i * piece, piece), piece)
@@ -128,7 +132,7 @@
             device_id=across, device_id_type=MESH,
         )
 
-    BOTH = ((0, 0), (0, 1), (1, 0), (1, 1))
+    BOTH = ((0, 0), (1, 0), (0, 1), (1, 1))
     LAST = ((0, 0), (1, 1))
 
     def first_sends(turn):
@@ -175,24 +179,21 @@
             load_rows(r, f).wait()
 
         def one(t, carry):
-            here = pl.ds(pl.multiple_of(t * tile, tile), tile)
-            for f in range(fields):
-                rows_in[r, f, :, here] = jnp.dot(
-                    perm, rows_in[r, f, :, here], preferred_element_type=F32
-                ).astype(BF16)
-            return carry
-
-        lax.fori_loop(0, states // tile, one, 0)
+            here = pl.ds(pl.multiple_of(t % (states // tile) * tile, tile), tile)
+            rows_in[part(r, t // (states // tile)), here] = jnp.dot(
+                perm, rows_in[part(r, t // (states // tile)), here], preferred_element_type=F32
+            ).astype(BF16)
+            return carry
+
+        lax.fori_loop(0, fields * (states // tile), one, 0)
 
     def permute(b):
-        tile = min(512, states)
+        tile = min(1024, states)
 
         def one(t, carry):
             here = pl.ds(pl.multiple_of(t * tile, tile), tile)
-            moved[core, b, here, :] = jnp.dot(
-                choose[here, :], jnp.concatenate([held[b, i].reshape(states, piece) for i in range(2)], axis=1),
-                preferred_element_type=F32,
-            ).astype(BF16)
+            block = jnp.concatenate([held[b, i].reshape(states, piece) for i in range(2)], axis=1)
+            moved[core, b, here, :] = jnp.dot(choose[here, :], block, preferred_element_type=F32).astype(BF16)
             return carry
 
         lax.fori_loop(0, states // tile, one, 0)
@@ -215,41 +216,36 @@
         root8 = tuple(jnp.broadcast_to(x, (SEGMENTS, width)) for x in root)
         jump = power(root, per_seg)
 
-        def one(r, carry):
-            for f in range(fields):
-                z[h, b, r, f] = jnp.dot(rows_in[r, f], moved[h, b], preferred_element_type=F32).astype(BF16)
-
-            def pairs(k):
-                both = pl.ds(k * SEGMENTS, 2 * SEGMENTS)
-                full = [z[h, b, r, f, both, :].astype(F32) for f in range(2)]
-                return [tuple(x[m * SEGMENTS:(m + 1) * SEGMENTS] for x in full) for m in range(2)]
-
-            low, high = pairs(0), pairs(per_seg - 2)
-            ahead = add(low[1], mul(root8, low[0]))
-            behind = add(high[0], mul(root8, high[1]))
-            for k in range(2, per_seg, 2):
-                low, high = pairs(k), pairs(per_seg - 2 - k)
-                ahead = add(low[0], mul(root8, ahead))
-                ahead = add(low[1], mul(root8, ahead))
-                behind = add(high[1], mul(root8, behind))
-                behind = add(high[0], mul(root8, behind))
+        z[h, b] = jnp.dot(rows_in[...], moved[h, b], preferred_element_type=F32).astype(BF16)
+
+        def pairs(r, k):
+            at = [(r * fields + f) * steps + k * SEGMENTS for f in range(2)]
+            full = [z[h, b, at[f]:at[f] + 2 * SEGMENTS, :].astype(F32) for f in range(2)]
+            return [tuple(x[m * SEGMENTS:(m + 1) * SEGMENTS] for x in full) for m in range(2)]
+
+        every = range(vectors)
+        low, high = [pairs(r, 0) for r in every], [pairs(r, per_seg - 2) for r in every]
+        ahead = [add(low[r][1], mul(root8, low[r][0])) for r in every]
+        behind = [add(high[r][0], mul(root8, high[r][1])) for r in every]
+        for k in range(2, per_seg, 2):
+            low, high = [pairs(r, k) for r in every], [pairs(r, per_seg - 2 - k) for r in every]
+            for m in range(2):
+                ahead = [add(low[r][m], mul(root8, ahead[r])) for r in every]
+                behind = [add(high[r][1 - m], mul(root8, behind[r])) for r in every]
+        slab = (h * half_modes + b * width) // lanes
+        row = lambda a, s: (a[0][s:s + 1], a[1][s:s + 1])
+        front, back = [row(ahead[r], 0) for r in every], [row(behind[r], SEGMENTS - 1) for r in every]
+        for s in range(1, SEGMENTS):
+            front = [add(row(ahead[r], s), mul(jump, front[r])) for r in every]
+            back = [add(row(behind[r], SEGMENTS - 1 - s), mul(jump, back[r])) for r in every]
+        for r in every:
             for c in range(2):
-                seg_out[h, b, r, 0, c] = ahead[c]
-                seg_out[h, b, r, 1, c] = behind[c]
-            row = lambda a, s: (a[0][s:s + 1], a[1][s:s + 1])
-            front, back = row(ahead, 0), row(behind, SEGMENTS - 1)
-            for s in range(1, SEGMENTS):
-                front = add(row(ahead, s), mul(jump, front))
-                back = add(row(behind, SEGMENTS - 1 - s), mul(jump, back))
-            slab = (h * half_modes + b * width) // lanes
-            for j in range(width // lanes):
-                cut = slice(j * lanes, (j + 1) * lanes)
-                for c in range(2):
-                    devs[slab + j, r, c:c + 1, :] = front[c][:, cut]
-                    devs[slab + j, r, 2 + c:3 + c, :] = back[c][:, cut]
-            return carry
-
-        lax.fori_loop(0, vectors, one, 0)
+                seg_out[h, b, r, 0, c] = ahead[r][c]
+                seg_out[h, b, r, 1, c] = behind[r][c]
+                for j in range(width // lanes):
+                    cut = slice(j * lanes, (j + 1) * lanes)
+                    devs[slab + j, c, r:r + 1, :] = front[r][c][:, cut]
+                    devs[slab + j, 2 + c, r:r + 1, :] = back[r][c][:, cut]
         store_z(h, b).start()
 
     def send_devs(e):
@@ -299,32 +295,40 @@
         whole = mul(power(hop, parts), root)
         square = mul(whole, whole)
         scale = mul(root, inverse_of((1.0 - square[0], -square[1])))
-        zero = jnp.zeros((1, lanes), F32)
-        for r in range(vectors):
-            row = lambda ref, d, c: (ref[d, r, c:c + 1, :], ref[d, r, c + 1:c + 2, :])
-
-            def scan(k, carry):
-                left, right = carry
-                d = parts - 1 - k
-                for c in range(2):
-                    edges[k, r, c:c + 1, :] = left[c]
-                    edges[d, r, 2 + c:3 + c, :] = right[c]
-                return add(row(devs_in, k, 0), mul(hop, left)), add(row(devs_in, d, 2), mul(hop, right))
-
-            all_left, all_right = lax.fori_loop(0, parts, scan, ((zero, zero), (zero, zero)))
-            start_term = mul(scale, sub(all_right, mul(whole, all_left)))
-            end_term = mul(scale, sub(all_left, mul(whole, all_right)))
-
-            def correct(k, carry):
-                start_term, end_term = carry
-                d = parts - 1 - k
-                left, right = sub(row(edges, k, 0), start_term), sub(row(edges, d, 2), end_term)
-                for c in range(2):
-                    edges[k, r, c:c + 1, :] = left[c]
-                    edges[d, r, 2 + c:3 + c, :] = right[c]
-                return mul(hop, start_term), mul(hop, end_term)
-
-            lax.fori_loop(0, parts, correct, (start_term, end_term))
+        zero = jnp.zeros((vectors, lanes), F32)
+
+        def each(step, carry):
+            if parts > 32:
+                return lax.fori_loop(0, parts, step, carry)
+            for k in range(parts):
+                carry = step(k, carry)
+            return carry
+
+        def row(ref, d, c):
+            return ref[d, c], ref[d, c + 1]
+
+        def scan(k, carry):
+            left, right = carry
+            d = parts - 1 - k
+            for c in range(2):
+                edges[k, c] = left[c]
+                edges[d, 2 + c] = right[c]
+            return add(row(devs_in, k, 0), mul(hop, left)), add(row(devs_in, d, 2), mul(hop, right))
+
+        all_left, all_right = each(scan, ((zero, zero), (zero, zero)))
+        start_term = mul(scale, sub(all_right, mul(whole, all_left)))
+        end_term = mul(scale, sub(all_left, mul(whole, all_right)))
+
+        def correct(k, carry):
+            start_term, end_term = carry
+            d = parts - 1 - k
+            left, right = sub(row(edges, k, 0), start_term), sub(row(edges, d, 2), end_term)
+            for c in range(2):
+                edges[k, c] = left[c]
+                edges[d, 2 + c] = right[c]
+            return mul(hop, start_term), mul(hop, end_term)
+
+        each(correct, (start_term, end_term))
 
     for r in range(vectors):
         for f in range(fields):
@@ -360,31 +364,15 @@
     first_sends(1)
     build_choose(2, 4)
     phase(0, 1)
-    order_rows(0)
+
+    def order_all(r, carry):
+        order_rows(r)
+        pl.when(r == 0)(lambda: phase(0, 2))
+        return carry
+
+    lax.fori_loop(0, vectors, order_all, 0)
     phase(1, 0)
-    for r in range(1, vectors):
-        order_rows(r)
-    phase(0, 2)
-    first_sends(2)
-    phase(1, 1)
     phase(0, 3)
-
-    def own_half(b):
-        hand_over(b, core).start()
-        store_moved(core, b).start()
-        to_modes(core, b)
-
-    def pair_half(b):
-        hand_over(b, other).wait_recv()
-        store_moved(other, b).start()
-        to_modes(other, b)
-
-    permute(group)
-    phase(1, 2)
-    own_half(group)
-    phase(2, 0)
-    pair_half(group)
-    phase(1, 3)
 
     def from_y(k, carry):
         source = chip_at(place + k)
@@ -392,19 +380,51 @@
             over_y(i, source, 1 - group).wait_recv()
         return carry
 
-    lax.fori_loop(1, chips, from_y, 0)
-    permute(1 - group)
-    phase(2, 1)
-    own_half(1 - group)
-    phase(2, 2)
-    pair_half(1 - group)
-    permute(2)
-    phase(2, 3)
-    permute(3)
-    own_half(2)
-    pair_half(2)
-    own_half(3)
-    pair_half(3)
+    plan = {
+        (0, 0): (lambda: phase(1, 1), lambda: first_sends(2)),
+        (0, 2): (lambda: phase(1, 2),),
+        (1, 0): (lambda: phase(1, 3), lambda: phase(2, 0)),
+        (1, 2): (lambda: phase(2, 1),),
+        (2, 0): (lambda: phase(2, 2),),
+        (2, 2): (lambda: phase(2, 3),),
+    }
+
+    def after(n, slot):
+        for (turn, at), acts in plan.items():
+            @pl.when((n * 3 + slot) == turn * 3 + at)
+            def _():
+                for act in acts:
+                    act()
+
+    def job(n, carry):
+        b = n + (1 - n // 2) * group * (1 - 2 * n)
+
+        @pl.when(n == 1)
+        def _():
+            lax.fori_loop(1, chips, from_y, 0)
+
+        permute(b)
+        hand_over(b, core).start()
+        store_moved(core, b).start()
+        after(n, 0)
+
+        def side(q, carry):
+            h = core + q * (1 - 2 * core)
+
+            @pl.when(q == 1)
+            def _():
+                hand_over(b, other).wait_recv()
+                store_moved(other, b).start()
+
+            to_modes(h, b)
+
+            after(n, 1 + q)
+            return carry
+
+        lax.fori_loop(0, 2, side, 0)
+        return carry
+
+    lax.fori_loop(0, BLOCKS, job, 0)
 
     others(owners, lambda e: send_devs(e).start())
 
@@ -448,22 +468,28 @@
 
 
 def backward_kernel(z_ref, seg_ref, edge_ref, mu_ref, moved_ref, out_ref, p_ref, u_ref, back_ref):
-    _, _, vectors, fields, steps, width = z_ref.shape
-    states = out_ref.shape[3]
+    vectors, fields, steps, tile = out_ref.shape
+    width = z_ref.shape[3]
+    half_modes = BLOCKS * width
     per_seg = steps // SEGMENTS
     slabs, lanes = edge_ref.shape[2], edge_ref.shape[5]
-    perm = time_order(steps, True)
-    for h in range(2):
+    step = pl.program_id(0)
+
+    def solve(h):
         root = decay_root(mu_ref[h, 0])
         root8 = tuple(jnp.broadcast_to(x, (SEGMENTS, width)) for x in root)
         jump = power(root, per_seg)
         square = mul(root, root)
         gain = mul(root, inverse_of((1.0 - square[0], -square[1])))
+        perm = time_order(steps, True)
+        columns = pl.ds(pl.multiple_of(h * half_modes + step * width, width), width)
 
         def edge(r, c):
-            return jnp.concatenate([edge_ref[h, 0, j, r, c:c + 1, :] for j in range(slabs)], axis=1)
-
-        for r in range(vectors):
+            return jnp.concatenate([edge_ref[h, 0, j, c, pl.ds(r, 1), :] for j in range(slabs)], axis=1)
+
+        every = range(vectors)
+        p, u = [], []
+        for r in every:
             row = lambda a, s: (seg_ref[h, 0, r, a, 0, s:s + 1, :], seg_ref[h, 0, r, a, 1, s:s + 1, :])
             lefts = [(edge(r, 0), edge(r, 1))]
             rights = [(edge(r, 2), edge(r, 3))]
@@ -474,49 +500,49 @@
             rights = rights[::-1]
             ends = [mul(gain, add(rights[s], mul(root, lefts[s + 1]))) for s in range(SEGMENTS)]
             stack = lambda rows: tuple(jnp.concatenate([x[c] for x in rows], axis=0) for c in range(2))
-            p = stack(lefts[:SEGMENTS])
-            for k in range(0, per_seg, 2):
-                both = pl.ds(k * SEGMENTS, 2 * SEGMENTS)
-                pair = [z_ref[h, 0, r, f, both, :].astype(F32) for f in range(2)]
-                for m in range(2):
-                    here = tuple(x[m * SEGMENTS:(m + 1) * SEGMENTS] for x in pair)
-                    p = add(here, mul(root8, p))
+            p.append(stack(lefts[:SEGMENTS]))
+            u.append(stack(ends))
+        for k in range(0, per_seg, 2):
+            at = [[(r * fields + f) * steps + k * SEGMENTS for f in range(2)] for r in every]
+            pair = [[z_ref[h, 0, a:a + 2 * SEGMENTS, :].astype(F32) for a in at[r]] for r in every]
+            for m in range(2):
+                for r in every:
+                    here = tuple(x[m * SEGMENTS:(m + 1) * SEGMENTS] for x in pair[r])
+                    p[r] = add(here, mul(root8, p[r]))
                     for c in range(2):
-                        p_ref[c, pl.ds((k + m) * SEGMENTS, SEGMENTS), :] = p[c]
-            u = stack(ends)
-            for k in range(per_seg - 2, -1, -2):
-                later = []
-                for m in (1, 0):
-                    here = pl.ds((k + m) * SEGMENTS, SEGMENTS)
-                    u = mul(root8, add((p_ref[0, here, :], p_ref[1, here, :]), u))
-                    later.append(u)
-                both = pl.ds(k * SEGMENTS, 2 * SEGMENTS)
+                        p_ref[r, c, pl.ds((k + m) * SEGMENTS, SEGMENTS), :] = p[r][c]
+        for k in range(per_seg - 2, -1, -2):
+            later = [[], []]
+            for m in (1, 0):
+                here = pl.ds((k + m) * SEGMENTS, SEGMENTS)
+                for r in every:
+                    u[r] = mul(root8, add((p_ref[r, 0, here, :], p_ref[r, 1, here, :]), u[r]))
+                later[m] = list(u)
+            both = pl.ds(k * SEGMENTS, 2 * SEGMENTS)
+            for r in every:
                 for c in range(2):
-                    u_ref[c, both, :] = jnp.concatenate([later[1][c], later[0][c]], axis=0).astype(BF16)
-            for c in range(2):
-                back_ref[r, c, :, h * width:(h + 1) * width] = jnp.dot(
-                    perm, u_ref[c], preferred_element_type=F32
-                ).astype(BF16)
-
-    tile = min(256, states)
-    step = pl.program_id(0)
-
-    def accumulate(first):
-        def one(t, carry):
-            here = pl.ds(pl.multiple_of(t * tile, tile), tile)
-            block = jnp.concatenate([moved_ref[h, 0, here, :] for h in range(2)], axis=1)
-            for r in range(vectors):
-                for f in range(fields):
-                    part = lax.dot_general(
-                        back_ref[r, f], block, (((1,), (1,)), ((), ())), preferred_element_type=F32
-                    )
-                    out_ref[r, f, :, here] = part if first else out_ref[r, f, :, here] + part
-            return carry
-
-        lax.fori_loop(0, states // tile, one, 0)
-
-    pl.when(step == 0)(lambda: accumulate(True))
-    pl.when(step > 0)(lambda: accumulate(False))
+                    at = (r * fields + c) * width
+                    u_ref[both, at:at + width] = jnp.concatenate(
+                        [later[0][r][c], later[1][r][c]], axis=0
+                    ).astype(BF16)
+        turned = jnp.dot(perm, u_ref[...], preferred_element_type=F32).astype(BF16)
+        for v in range(vectors * fields):
+            back_ref[pl.ds(v * steps, steps), columns] = turned[:, v * width:(v + 1) * width]
+
+    @pl.when(step < BLOCKS)
+    def _():
+        def one(h, carry):
+            solve(h)
+            return carry
+
+        lax.fori_loop(0, 2, one, 0)
+
+    @pl.when(step >= BLOCKS)
+    def _():
+        block = jnp.concatenate([moved_ref[h, b] for h in range(2) for b in range(BLOCKS)], axis=1)
+        out_ref[...] = lax.dot_general(
+            back_ref[...], block, (((1,), (1,)), ((), ())), preferred_element_type=F32
+        ).reshape(out_ref.shape)
 
 
 def on_device(residual, eigenbasis, eigenvalues, node_order):
@@ -535,9 +561,9 @@
         functools.partial(forward_kernel, chips),
         out_shape=[
             jax.ShapeDtypeStruct((2, BLOCKS, states, width), BF16),
-            jax.ShapeDtypeStruct((2, BLOCKS, vectors, fields, steps, width), BF16),
+            jax.ShapeDtypeStruct((2, BLOCKS, vectors * fields * steps, width), BF16),
             jax.ShapeDtypeStruct((2, BLOCKS, vectors, 2, 2, SEGMENTS, width), F32),
-            jax.ShapeDtypeStruct((owners, vectors, 4, lanes), F32),
+            jax.ShapeDtypeStruct((owners, 4, vectors, lanes), F32),
         ],
         in_specs=[anyspace, vm, vm, vm, anyspace],
         out_specs=[anyspace, anyspace, vm, vm],
@@ -545,12 +571,12 @@
             pltpu.VMEM((BLOCKS, 2, chips, 2 * rows, width // 2), BF16),
             pltpu.VMEM((states, states), BF16),
             pltpu.VMEM((2, BLOCKS, states, width), BF16),
-            pltpu.VMEM((vectors, fields, steps, states), BF16),
-            pltpu.VMEM((2, BLOCKS, vectors, fields, steps, width), BF16),
-            pltpu.VMEM((owners, vectors, 4, lanes), F32),
-            pltpu.VMEM((parts, vectors, 4, lanes), F32),
-            pltpu.VMEM((parts, vectors, 4, lanes), F32),
-            pltpu.VMEM((owners, vectors, 4, lanes), F32),
+            pltpu.VMEM((vectors * fields * steps, states), BF16),
+            pltpu.VMEM((2, BLOCKS, vectors * fields * steps, width), BF16),
+            pltpu.VMEM((owners, 4, vectors, lanes), F32),
+            pltpu.VMEM((parts, 4, vectors, lanes), F32),
+            pltpu.VMEM((parts, 4, vectors, lanes), F32),
+            pltpu.VMEM((owners, 4, vectors, lanes), F32),
             dma((8 + vectors * fields + 4 * BLOCKS,)),
             dma((8,)), dma((8,)),
             dma((12, chips // 2)), dma((12, chips // 2)),
@@ -559,31 +585,35 @@
             dma((owners,)), dma((parts,)), dma((parts,)), dma((owners,)),
         ],
         compiler_params=pltpu.CompilerParams(
-            collective_id=0, has_side_effects=True, vmem_limit_bytes=50 * 1024 * 1024
+            collective_id=0, has_side_effects=True, vmem_limit_bytes=VMEM_BYTES
         ),
         name="forward",
     )(eigenbasis, node_order.reshape(1, states), mu, eigenvalues.reshape(owners, 1, lanes), residual)
 
+    tiles = 4
+    tile = states // tiles
+    solved = lambda i: jnp.minimum(i, BLOCKS - 1)
+    written = lambda i: jnp.maximum(i - BLOCKS, 0)
     return pl.pallas_call(
         backward_kernel,
-        grid=(BLOCKS,),
+        grid=(BLOCKS + tiles,),
         in_specs=[
-            pl.BlockSpec((2, 1, vectors, fields, steps, width), lambda b: (0, b, 0, 0, 0, 0)),
-            pl.BlockSpec((2, 1, vectors, 2, 2, SEGMENTS, width), lambda b: (0, b, 0, 0, 0, 0, 0)),
-            pl.BlockSpec((2, 1, slabs, vectors, 4, lanes), lambda b: (0, b, 0, 0, 0, 0)),
-            pl.BlockSpec((2, 1, 1, width), lambda b: (0, b, 0, 0)),
-            pl.BlockSpec((2, 1, states, width), lambda b: (0, b, 0, 0)),
+            pl.BlockSpec((2, 1, vectors * fields * steps, width), lambda i: (0, solved(i), 0, 0)),
+            pl.BlockSpec((2, 1, vectors, 2, 2, SEGMENTS, width), lambda i: (0, solved(i), 0, 0, 0, 0, 0)),
+            pl.BlockSpec((2, 1, slabs, 4, vectors, lanes), lambda i: (0, solved(i), 0, 0, 0, 0)),
+            pl.BlockSpec((2, 1, 1, width), lambda i: (0, solved(i), 0, 0)),
+            pl.BlockSpec((2, BLOCKS, tile, width), lambda i: (0, 0, written(i), 0)),
         ],
-        out_specs=pl.BlockSpec((vectors, fields, steps, states), lambda b: (0, 0, 0, 0)),
+        out_specs=pl.BlockSpec((vectors, fields, steps, tile), lambda i: (0, 0, 0, written(i))),
         out_shape=jax.ShapeDtypeStruct((vectors, fields, steps, states), F32),
         scratch_shapes=[
-            pltpu.VMEM((2, steps, width), F32),
-            pltpu.VMEM((2, steps, width), BF16),
-            pltpu.VMEM((vectors, fields, steps, 2 * width), BF16),
+            pltpu.VMEM((vectors, 2, steps, width), F32),
+            pltpu.VMEM((steps, vectors * fields * width), BF16),
+            pltpu.VMEM((vectors * fields * steps, modes), BF16),
         ],
-        compiler_params=pltpu.CompilerParams(vmem_limit_bytes=50 * 1024 * 1024),
+        compiler_params=pltpu.CompilerParams(vmem_limit_bytes=VMEM_BYTES),
         name="backward",
-    )(z, seg, edge.reshape(2, BLOCKS, slabs, vectors, 4, lanes), mu, moved)
+    )(z, seg, edge.reshape(2, BLOCKS, slabs, 4, vectors, lanes), mu, moved)
 
 
 def solution(mesh):

time: 102 us -> 87.6 us (0.86)
  Pallas kernels: 98.4 us -> 87.3 us
  local copies, waits for them, and re-layouts: 3.13 us -> 0 us
    pallas_call x1, Pallas kernels: 26.4 us -> 19.9 us  [on_device(): pl.pallas_call(backward_kernel, grid=(BLOCKS + tiles,), in_specs=[pl.Bloc...]
    pallas_call x1, Pallas kernels: 72 us -> 67.4 us  [on_device(): pl.pallas_call(functools.partial(forward_kernel, chips), out_shape=[jax.S...]
    unnamed x8 -> x0, local copies, waits for them, and re-layouts: 3.13 us -> none
where the time goes in v2:
time: 87.6 us; the launch traced here: 87.3 us
  Pallas kernels  87.3 us (100%)
    pallas_call x1, Pallas kernels, on_device(): pl.pallas_call(functools.partial(forward_kernel, chips), out_shape=[jax.S...  67.4 us
    pallas_call x1, Pallas kernels, on_device(): pl.pallas_call(backward_kernel, grid=(BLOCKS + tiles,), in_specs=[pl.Bloc...  19.9 us

profile of v2, /device:TPU:0, one launch (start us, length us, event | category | flops | bytes accessed | tf_op | source)
XLA Modules:
  0.0 87.3 jit_solution(5042980290610288704)
XLA Ops:
  0.0 67.4 %forward.1 = (bf16[2,4,2048,256]{3,2,1,0:T(8,128)(2,1)}, bf16[2,4,1024,256]{3,2,1,0:T(8,128)(2,1)}, f32[2,4,2,2,2,8,256]{6,5,4,3,2,1,0:T(8,128)}, f32[16,4,2,128]{3,2,1,0:T(2,128)}) custom-call(bf16[128,2048]{1,0:T(8,128)(2,1)} %basis_ref.1, s32[1,2048]{1,0:T(1,128)} %bitcast.8, f32[2,4,1,256]{3,2,1,0:T(1,128)} %bitcast.4, f32[16,1,128]{2,1,0:T(1,128)} %bitcast.5, ...), custom_call_target="tpu_custom_call" | custom-call | tf_op jit(solution)/shard_map/forward/pallas_call | solution.py:560
  67.4 19.9 %backward.1 = f32[2,2,256,2048]{3,2,1,0:T(8,128)} custom-call(bf16[2,4,1024,256]{3,2,1,0:T(8,128)(2,1)} %get-tuple-element.9.z_ref, f32[2,4,2,2,2,8,256]{6,5,4,3,2,1,0:T(8,128)} %get-tuple-element.10.seg_ref, f32[2,4,2,4,2,128]{5,4,3,2,1,0:T(2,128)} %bitcast.7, f32[2,4,1,256]{3,2,1,0:T(1,128)} %bitcast.6, bf16[2,4,2048,256]{3,2,1,0:T(8,128)(2,1)} %get-tuple-element.12.moved_ref), custom_call_target="tpu_custom_call" | custom-call | tf_op jit(solution)/shard_map/backward/pallas_call | solution.py:597

commit v3 on v2

--- a/solution.py
+++ b/solution.py
@@ -62,9 +62,9 @@
 
 def forward_kernel(
     chips, basis_ref, node_ref, mu_ref, unit_mu_ref, residual_ref,
-    moved_out, z_out, seg_out, edge_out,
-    held, choose, moved, rows_in, z, devs, devs_in, edges, edges_in,
-    local_sem, pair_send, pair_recv, ring_send, ring_recv, y_send, y_recv,
+    moved_out, back_out,
+    held, choose, moved, rows_in, z, seg, p_part, u_part, devs, devs_in, edges, edges_in,
+    local_sem, pair_send, pair_recv, direct_send, direct_recv, ring_send, ring_recv, y_send, y_recv,
     block_send, block_recv, dev_send, dev_recv, edge_send, edge_recv,
 ):
     vectors, fields, steps, states = residual_ref.shape
@@ -73,6 +73,7 @@
     piece = width // 2
     half_modes = modes // 2
     owners, lanes = devs.shape[0], devs.shape[3]
+    slabs = width // lanes
     parts = 2 * chips
     half = chips // 2
     per_seg = steps // SEGMENTS
@@ -135,13 +136,42 @@
     BOTH = ((0, 0), (1, 0), (0, 1), (1, 1))
     LAST = ((0, 0), (1, 1))
 
+    def direct(d, i, w, source, towards):
+        columns = pl.ds(pl.multiple_of(w * half_modes + group * width + i * piece, piece), piece)
+        return pltpu.make_async_remote_copy(
+            src_ref=basis_ref.at[:, columns],
+            dst_ref=held.at[group, i, source, pl.ds(pl.multiple_of(towards * rows, rows), rows)],
+            send_sem=direct_send.at[d * 2 + i, w], recv_sem=direct_recv.at[d * 2 + i, towards],
+            device_id={"tm": targets[d] - core + w}, device_id_type=MESH,
+        )
+
+    def direct_sends():
+        for d, i in (BOTH if half > 1 else LAST):
+            for w in range(2):
+                direct(d, i, w, chip, core).start()
+
     def first_sends(turn):
         for d, i in (BOTH if half > 1 else LAST):
             ring(turn, 1, d, i, 0).start()
 
+    def arrived(turn, s, d, i):
+        if turn or (isinstance(s, int) and s > 1):
+            ring(turn, s, d, i, 1).wait_recv()
+            return
+        source = chip_at(place - s) if d == 0 else chip_at(place + s)
+
+        @pl.when(s == 1)
+        def _():
+            for w in range(2):
+                direct(d, i, 0, source, w).wait_recv()
+
+        @pl.when(s > 1)
+        def _():
+            ring(turn, s, d, i, 1).wait_recv()
+
     def event(turn, s, kind):
         for d, i in (LAST if kind == "last" else BOTH):
-            ring(turn, s, d, i, 1).wait_recv()
+            arrived(turn, s, d, i)
             if kind == "mid" or (kind == "next_last" and i == d):
                 ring(turn, s + 1, d, i, 0).start()
             if turn == 0:
@@ -188,20 +218,21 @@
         lax.fori_loop(0, fields * (states // tile), one, 0)
 
     def permute(b):
-        tile = min(1024, states)
+        tile = states // 2
 
         def one(t, carry):
             here = pl.ds(pl.multiple_of(t * tile, tile), tile)
             block = jnp.concatenate([held[b, i].reshape(states, piece) for i in range(2)], axis=1)
             moved[core, b, here, :] = jnp.dot(choose[here, :], block, preferred_element_type=F32).astype(BF16)
-            return carry
-
-        lax.fori_loop(0, states // tile, one, 0)
-
-    def hand_over(b, side):
-        ref = moved.at[side, b]
-        return pltpu.make_async_remote_copy(
-            src_ref=ref, dst_ref=ref, send_sem=block_send.at[b], recv_sem=block_recv.at[b],
+            hand_over(b, core, t).start()
+            return carry
+
+        lax.fori_loop(0, 2, one, 0)
+
+    def hand_over(b, side, t):
+        ref = moved.at[side, b, pl.ds(pl.multiple_of(t * (states // 2), states // 2), states // 2)]
+        return pltpu.make_async_remote_copy(
+            src_ref=ref, dst_ref=ref, send_sem=block_send.at[b, t], recv_sem=block_recv.at[b, t],
             device_id=pair, device_id_type=MESH,
         )
 
@@ -209,7 +240,7 @@
         return pltpu.make_async_copy(moved.at[h, b], moved_out.at[h, b], local_sem.at[8 + vectors * fields + h * BLOCKS + b])
 
     def store_z(h, b):
-        return pltpu.make_async_copy(z.at[h, b], z_out.at[h, b], local_sem.at[8 + vectors * fields + (2 + h) * BLOCKS + b])
+        return pltpu.make_async_copy(z.at[h, b], back_out.at[h, b], local_sem.at[8 + vectors * fields + (2 + h) * BLOCKS + b])
 
     def to_modes(h, b):
         root = decay_root(mu_ref[h, b])
@@ -240,13 +271,12 @@
             back = [add(row(behind[r], SEGMENTS - 1 - s), mul(jump, back[r])) for r in every]
         for r in every:
             for c in range(2):
-                seg_out[h, b, r, 0, c] = ahead[r][c]
-                seg_out[h, b, r, 1, c] = behind[r][c]
+                seg[h, b, r, 0, c] = ahead[r][c]
+                seg[h, b, r, 1, c] = behind[r][c]
                 for j in range(width // lanes):
                     cut = slice(j * lanes, (j + 1) * lanes)
                     devs[slab + j, c, r:r + 1, :] = front[r][c][:, cut]
                     devs[slab + j, 2 + c, r:r + 1, :] = back[r][c][:, cut]
-        store_z(h, b).start()
 
     def send_devs(e):
         return pltpu.make_async_remote_copy(
@@ -330,167 +360,22 @@
 
         each(correct, (start_term, end_term))
 
-    for r in range(vectors):
-        for f in range(fields):
-            load_rows(r, f).start()
-    for b in range(BLOCKS):
-        for i in range(2):
-            own_rows(b, i).start()
-
-    barrier = pltpu.get_barrier_semaphore()
-
-    def greet(k, carry):
-        pl.semaphore_signal(barrier, inc=1, device_id={"tm": (me + k) % parts}, device_id_type=MESH)
-        return carry
-
-    lax.fori_loop(1, parts, greet, 0)
-    pl.semaphore_signal(barrier, inc=1, device_id=across, device_id_type=MESH)
-    pl.semaphore_wait(barrier, parts)
-
-    for b in order:
-        for i in range(2):
-            pair_rows(b, i, other, core).start()
-    for b in ring_blocks[:1]:
-        for i in range(2):
-            own_rows(b, i).wait()
-            pair_rows(b, i, core, other).wait_recv()
-    first_sends(0)
-    build_choose(0, 2)
-    for b in order[1:]:
-        for i in range(2):
-            own_rows(b, i).wait()
-            pair_rows(b, i, core, other).wait_recv()
-    phase(0, 0)
-    first_sends(1)
-    build_choose(2, 4)
-    phase(0, 1)
-
-    def order_all(r, carry):
-        order_rows(r)
-        pl.when(r == 0)(lambda: phase(0, 2))
-        return carry
-
-    lax.fori_loop(0, vectors, order_all, 0)
-    phase(1, 0)
-    phase(0, 3)
-
-    def from_y(k, carry):
-        source = chip_at(place + k)
-        for i in range(2):
-            over_y(i, source, 1 - group).wait_recv()
-        return carry
-
-    plan = {
-        (0, 0): (lambda: phase(1, 1), lambda: first_sends(2)),
-        (0, 2): (lambda: phase(1, 2),),
-        (1, 0): (lambda: phase(1, 3), lambda: phase(2, 0)),
-        (1, 2): (lambda: phase(2, 1),),
-        (2, 0): (lambda: phase(2, 2),),
-        (2, 2): (lambda: phase(2, 3),),
-    }
-
-    def after(n, slot):
-        for (turn, at), acts in plan.items():
-            @pl.when((n * 3 + slot) == turn * 3 + at)
-            def _():
-                for act in acts:
-                    act()
-
-    def job(n, carry):
-        b = n + (1 - n // 2) * group * (1 - 2 * n)
-
-        @pl.when(n == 1)
-        def _():
-            lax.fori_loop(1, chips, from_y, 0)
-
-        permute(b)
-        hand_over(b, core).start()
-        store_moved(core, b).start()
-        after(n, 0)
-
-        def side(q, carry):
-            h = core + q * (1 - 2 * core)
-
-            @pl.when(q == 1)
-            def _():
-                hand_over(b, other).wait_recv()
-                store_moved(other, b).start()
-
-            to_modes(h, b)
-
-            after(n, 1 + q)
-            return carry
-
-        lax.fori_loop(0, 2, side, 0)
-        return carry
-
-    lax.fori_loop(0, BLOCKS, job, 0)
-
-    others(owners, lambda e: send_devs(e).start())
-
-    def settle():
-        devs_in[me] = devs[me]
-        others(parts, lambda d: devs_from(d).wait_recv())
-        couple()
-        others(parts, lambda d: send_edges(d).start())
-        edges_in[me] = edges[me]
-
-    if_owner(settle)
-    others(owners, lambda e: edges_from(e).wait_recv())
-    edge_out[...] = edges_in[...]
-
-    others(owners, lambda e: send_devs(e).wait_send())
-    if_owner(lambda: others(parts, lambda d: send_edges(d).wait_send()))
-    for b in order:
-        for i in range(2):
-            pair_rows(b, i, other, core).wait_send()
-        hand_over(b, core).wait_send()
-        for h in range(2):
-            store_moved(h, b).wait()
-            store_z(h, b).wait()
-    for turn in range(3):
-        def drain(s, carry):
-            for d, i in BOTH:
-                ring(turn, s, d, i, 0).wait_send()
-            return carry
-
-        lax.fori_loop(1, half, drain, 0)
-        for d, i in LAST:
-            ring(turn, half, d, i, 0).wait_send()
-
-    def y_drain(k, carry):
-        source = chip_at(place + k)
-        for i in range(2):
-            over_y(i, source, group).wait_send()
-        return carry
-
-    lax.fori_loop(1, chips, y_drain, 0)
-
-
-def backward_kernel(z_ref, seg_ref, edge_ref, mu_ref, moved_ref, out_ref, p_ref, u_ref, back_ref):
-    vectors, fields, steps, tile = out_ref.shape
-    width = z_ref.shape[3]
-    half_modes = BLOCKS * width
-    per_seg = steps // SEGMENTS
-    slabs, lanes = edge_ref.shape[2], edge_ref.shape[5]
-    step = pl.program_id(0)
-
-    def solve(h):
-        root = decay_root(mu_ref[h, 0])
+    def solve(h, b):
+        root = decay_root(mu_ref[h, b])
         root8 = tuple(jnp.broadcast_to(x, (SEGMENTS, width)) for x in root)
         jump = power(root, per_seg)
         square = mul(root, root)
         gain = mul(root, inverse_of((1.0 - square[0], -square[1])))
         perm = time_order(steps, True)
-        columns = pl.ds(pl.multiple_of(h * half_modes + step * width, width), width)
+        slab = (h * half_modes + b * width) // lanes
 
         def edge(r, c):
-            return jnp.concatenate([edge_ref[h, 0, j, c, pl.ds(r, 1), :] for j in range(slabs)], axis=1)
+            return jnp.concatenate([edges_in[slab + j, c, r:r + 1, :] for j in range(width // lanes)], axis=1)
 
         every = range(vectors)
         p, u = [], []
         for r in every:
-            row = lambda a, s: (seg_ref[h, 0, r, a, 0, s:s + 1, :], seg_ref[h, 0, r, a, 1, s:s + 1, :])
+            row = lambda a, s: (seg[h, b, r, a, 0, s:s + 1, :], seg[h, b, r, a, 1, s:s + 1, :])
             lefts = [(edge(r, 0), edge(r, 1))]
             rights = [(edge(r, 2), edge(r, 3))]
             for s in range(SEGMENTS):
@@ -504,45 +389,206 @@
             u.append(stack(ends))
         for k in range(0, per_seg, 2):
             at = [[(r * fields + f) * steps + k * SEGMENTS for f in range(2)] for r in every]
-            pair = [[z_ref[h, 0, a:a + 2 * SEGMENTS, :].astype(F32) for a in at[r]] for r in every]
+            pair = [[z[h, b, a:a + 2 * SEGMENTS, :].astype(F32) for a in at[r]] for r in every]
             for m in range(2):
                 for r in every:
                     here = tuple(x[m * SEGMENTS:(m + 1) * SEGMENTS] for x in pair[r])
                     p[r] = add(here, mul(root8, p[r]))
                     for c in range(2):
-                        p_ref[r, c, pl.ds((k + m) * SEGMENTS, SEGMENTS), :] = p[r][c]
+                        p_part[r, c, pl.ds((k + m) * SEGMENTS, SEGMENTS), :] = p[r][c]
         for k in range(per_seg - 2, -1, -2):
             later = [[], []]
             for m in (1, 0):
                 here = pl.ds((k + m) * SEGMENTS, SEGMENTS)
                 for r in every:
-                    u[r] = mul(root8, add((p_ref[r, 0, here, :], p_ref[r, 1, here, :]), u[r]))
+                    u[r] = mul(root8, add((p_part[r, 0, here, :], p_part[r, 1, here, :]), u[r]))
                 later[m] = list(u)
             both = pl.ds(k * SEGMENTS, 2 * SEGMENTS)
             for r in every:
                 for c in range(2):
                     at = (r * fields + c) * width
-                    u_ref[both, at:at + width] = jnp.concatenate(
+                    u_part[both, at:at + width] = jnp.concatenate(
                         [later[0][r][c], later[1][r][c]], axis=0
                     ).astype(BF16)
-        turned = jnp.dot(perm, u_ref[...], preferred_element_type=F32).astype(BF16)
+        turned = jnp.dot(perm, u_part[...], preferred_element_type=F32).astype(BF16)
         for v in range(vectors * fields):
-            back_ref[pl.ds(v * steps, steps), columns] = turned[:, v * width:(v + 1) * width]
-
-    @pl.when(step < BLOCKS)
-    def _():
+            z[h, b, v * steps:(v + 1) * steps, :] = turned[:, v * width:(v + 1) * width]
+
+    for r in range(vectors):
+        for f in range(fields):
+            load_rows(r, f).start()
+    for b in range(BLOCKS):
+        for i in range(2):
+            own_rows(b, i).start()
+
+    barrier = pltpu.get_barrier_semaphore()
+
+    def greet(k, carry):
+        pl.semaphore_signal(barrier, inc=1, device_id={"tm": (me + k) % parts}, device_id_type=MESH)
+        return carry
+
+    lax.fori_loop(1, parts, greet, 0)
+    pl.semaphore_signal(barrier, inc=1, device_id=across, device_id_type=MESH)
+    pl.semaphore_wait(barrier, parts)
+
+    direct_sends()
+    for b in order:
+        for i in range(2):
+            pair_rows(b, i, other, core).start()
+    build_choose(0, 2)
+    for b in order:
+        for i in range(2):
+            own_rows(b, i).wait()
+            pair_rows(b, i, core, other).wait_recv()
+    phase(0, 0)
+    first_sends(1)
+    build_choose(2, 4)
+    phase(0, 1)
+
+    def order_all(r, carry):
+        order_rows(r)
+        pl.when(r == 0)(lambda: phase(0, 2))
+        return carry
+
+    lax.fori_loop(0, vectors, order_all, 0)
+    phase(1, 0)
+    phase(0, 3)
+
+    def from_y(k, carry):
+        source = chip_at(place + k)
+        for i in range(2):
+            over_y(i, source, 1 - group).wait_recv()
+        return carry
+
+    plan = {
+        (0, 0): (lambda: phase(1, 1), lambda: first_sends(2)),
+        (0, 2): (lambda: phase(1, 2),),
+        (1, 0): (lambda: phase(1, 3), lambda: phase(2, 0)),
+        (1, 2): (lambda: phase(2, 1),),
+        (2, 0): (lambda: phase(2, 2),),
+        (2, 2): (lambda: phase(2, 3),),
+    }
+
+    def after(n, slot):
+        for (turn, at), acts in plan.items():
+            @pl.when((n * 3 + slot) == turn * 3 + at)
+            def _():
+                for act in acts:
+                    act()
+
+    def block_at(n):
+        return n + (1 - n // 2) * group * (1 - 2 * n)
+
+    def each_slab(b, act):
+        def body(q, carry):
+            e = ((q // slabs) * half_modes + b * width) // lanes + q % slabs
+            pl.when(e != me)(lambda: act(e))
+            return carry
+
+        lax.fori_loop(0, 2 * slabs, body, 0)
+
+    def settle(b):
+        @pl.when((me < owners) & ((me * lanes) % half_modes // width == b))
+        def _():
+            devs_in[me] = devs[me]
+            others(parts, lambda d: devs_from(d).wait_recv())
+            couple()
+            others(parts, lambda d: send_edges(d).start())
+            edges_in[me] = edges[me]
+
+    def finish(b):
+        each_slab(b, lambda e: edges_from(e).wait_recv())
+
         def one(h, carry):
-            solve(h)
+            solve(h, b)
+            store_z(h, b).start()
             return carry
 
         lax.fori_loop(0, 2, one, 0)
 
-    @pl.when(step >= BLOCKS)
-    def _():
-        block = jnp.concatenate([moved_ref[h, b] for h in range(2) for b in range(BLOCKS)], axis=1)
-        out_ref[...] = lax.dot_general(
-            back_ref[...], block, (((1,), (1,)), ((), ())), preferred_element_type=F32
-        ).reshape(out_ref.shape)
+    def job(n, carry):
+        b, last = block_at(n), block_at(n - 1)
+
+        @pl.when(n < BLOCKS)
+        def _():
+            @pl.when(n == 1)
+            def _():
+                lax.fori_loop(1, chips, from_y, 0)
+
+            permute(b)
+            store_moved(core, b).start()
+            after(n, 0)
+
+        @pl.when(n > 0)
+        def _():
+            settle(last)
+
+        @pl.when(n < BLOCKS)
+        def _():
+            def side(q, carry):
+                h = core + q * (1 - 2 * core)
+
+                @pl.when(q == 1)
+                def _():
+                    for t in range(2):
+                        hand_over(b, other, t).wait_recv()
+                    store_moved(other, b).start()
+
+                to_modes(h, b)
+                pl.when(q == 1)(lambda: each_slab(b, lambda e: send_devs(e).start()))
+                after(n, 1 + q)
+                return carry
+
+            lax.fori_loop(0, 2, side, 0)
+
+        @pl.when(n > 0)
+        def _():
+            finish(last)
+
+        return carry
+
+    lax.fori_loop(0, BLOCKS + 1, job, 0)
+
+    others(owners, lambda e: send_devs(e).wait_send())
+    if_owner(lambda: others(parts, lambda d: send_edges(d).wait_send()))
+    for b in order:
+        for i in range(2):
+            pair_rows(b, i, other, core).wait_send()
+        for t in range(2):
+            hand_over(b, core, t).wait_send()
+        for h in range(2):
+            store_moved(h, b).wait()
+            store_z(h, b).wait()
+    for turn in range(3):
+        def drain(s, carry):
+            for d, i in BOTH:
+                ring(turn, s, d, i, 0).wait_send()
+            return carry
+
+        lax.fori_loop(1 if turn else 2, half, drain, 0)
+        if turn or half > 1:
+            for d, i in LAST:
+                ring(turn, half, d, i, 0).wait_send()
+    for d, i in (BOTH if half > 1 else LAST):
+        for w in range(2):
+            direct(d, i, w, chip, core).wait_send()
+
+    def y_drain(k, carry):
+        source = chip_at(place + k)
+        for i in range(2):
+            over_y(i, source, group).wait_send()
+        return carry
+
+    lax.fori_loop(1, chips, y_drain, 0)
+
+
+def backward_kernel(back_ref, moved_ref, out_ref):
+    halves = [(h, b) for h in range(2) for b in range(BLOCKS)]
+    back = jnp.concatenate([back_ref[h, b] for h, b in halves], axis=1)
+    block = jnp.concatenate([moved_ref[h, b] for h, b in halves], axis=1)
+    out_ref[...] = lax.dot_general(
+        back, block, (((1,), (1,)), ((), ())), preferred_element_type=F32
+    ).reshape(out_ref.shape)
 
 
 def on_device(residual, eigenbasis, eigenvalues, node_order):
@@ -553,35 +599,36 @@
     width = modes // (2 * BLOCKS)
     owners = min(parts, modes // 128)
     lanes = modes // owners
-    slabs = width // lanes
     vm, anyspace = pl.BlockSpec(memory_space=pltpu.VMEM), pl.BlockSpec(memory_space=pl.ANY)
     dma = pltpu.SemaphoreType.DMA
     mu = eigenvalues.reshape(2, BLOCKS, 1, width)
-    moved, z, seg, edge = pl.pallas_call(
+    moved, back = pl.pallas_call(
         functools.partial(forward_kernel, chips),
         out_shape=[
             jax.ShapeDtypeStruct((2, BLOCKS, states, width), BF16),
             jax.ShapeDtypeStruct((2, BLOCKS, vectors * fields * steps, width), BF16),
-            jax.ShapeDtypeStruct((2, BLOCKS, vectors, 2, 2, SEGMENTS, width), F32),
-            jax.ShapeDtypeStruct((owners, 4, vectors, lanes), F32),
         ],
         in_specs=[anyspace, vm, vm, vm, anyspace],
-        out_specs=[anyspace, anyspace, vm, vm],
+        out_specs=[anyspace, anyspace],
         scratch_shapes=[
             pltpu.VMEM((BLOCKS, 2, chips, 2 * rows, width // 2), BF16),
             pltpu.VMEM((states, states), BF16),
             pltpu.VMEM((2, BLOCKS, states, width), BF16),
             pltpu.VMEM((vectors * fields * steps, states), BF16),
             pltpu.VMEM((2, BLOCKS, vectors * fields * steps, width), BF16),
+            pltpu.VMEM((2, BLOCKS, vectors, 2, 2, SEGMENTS, width), F32),
+            pltpu.VMEM((vectors, 2, steps, width), F32),
+            pltpu.VMEM((steps, vectors * fields * width), BF16),
             pltpu.VMEM((owners, 4, vectors, lanes), F32),
             pltpu.VMEM((parts, 4, vectors, lanes), F32),
             pltpu.VMEM((parts, 4, vectors, lanes), F32),
             pltpu.VMEM((owners, 4, vectors, lanes), F32),
             dma((8 + vectors * fields + 4 * BLOCKS,)),
             dma((8,)), dma((8,)),
+            dma((4, 2)), dma((4, 2)),
             dma((12, chips // 2)), dma((12, chips // 2)),
             dma((2, chips)), dma((2, chips)),
-            dma((BLOCKS,)), dma((BLOCKS,)),
+            dma((BLOCKS, 2)), dma((BLOCKS, 2)),
             dma((owners,)), dma((parts,)), dma((parts,)), dma((owners,)),
         ],
         compiler_params=pltpu.CompilerParams(
@@ -592,28 +639,18 @@
 
     tiles = 4
     tile = states // tiles
-    solved = lambda i: jnp.minimum(i, BLOCKS - 1)
-    written = lambda i: jnp.maximum(i - BLOCKS, 0)
     return pl.pallas_call(
         backward_kernel,
-        grid=(BLOCKS + tiles,),
+        grid=(tiles,),
         in_specs=[
-            pl.BlockSpec((2, 1, vectors * fields * steps, width), lambda i: (0, solved(i), 0, 0)),
-            pl.BlockSpec((2, 1, vectors, 2, 2, SEGMENTS, width), lambda i: (0, solved(i), 0, 0, 0, 0, 0)),
-            pl.BlockSpec((2, 1, slabs, 4, vectors, lanes), lambda i: (0, solved(i), 0, 0, 0, 0)),
-            pl.BlockSpec((2, 1, 1, width), lambda i: (0, solved(i), 0, 0)),
-            pl.BlockSpec((2, BLOCKS, tile, width), lambda i: (0, 0, written(i), 0)),
+            pl.BlockSpec((2, BLOCKS, vectors * fields * steps, width), lambda i: (0, 0, 0, 0)),
+            pl.BlockSpec((2, BLOCKS, tile, width), lambda i: (0, 0, i, 0)),
         ],
-        out_specs=pl.BlockSpec((vectors, fields, steps, tile), lambda i: (0, 0, 0, written(i))),
+        out_specs=pl.BlockSpec((vectors, fields, steps, tile), lambda i: (0, 0, 0, i)),
         out_shape=jax.ShapeDtypeStruct((vectors, fields, steps, states), F32),
-        scratch_shapes=[
-            pltpu.VMEM((vectors, 2, steps, width), F32),
-            pltpu.VMEM((steps, vectors * fields * width), BF16),
-            pltpu.VMEM((vectors * fields * steps, modes), BF16),
-        ],
         compiler_params=pltpu.CompilerParams(vmem_limit_bytes=VMEM_BYTES),
         name="backward",
-    )(z, seg, edge.reshape(2, BLOCKS, slabs, 4, vectors, lanes), mu, moved)
+    )(back, moved)
 
 
 def solution(mesh):

time: 87.6 us -> 85.7 us (0.978)
  Pallas kernels: 87.3 us -> 85.5 us
    pallas_call x1, Pallas kernels: 19.9 us -> 13.6 us  [on_device(): pl.pallas_call(backward_kernel, grid=(tiles,), in_specs=[pl.BlockSpec((2,...]
    pallas_call x1, Pallas kernels: 67.4 us -> 71.8 us  [on_device(): pl.pallas_call(functools.partial(forward_kernel, chips), out_shape=[jax.S...]
where the time goes in v3:
time: 85.7 us; the launch traced here: 85.5 us
  Pallas kernels  85.5 us (100%)
    pallas_call x1, Pallas kernels, on_device(): pl.pallas_call(functools.partial(forward_kernel, chips), out_shape=[jax.S...  71.8 us
    pallas_call x1, Pallas kernels, on_device(): pl.pallas_call(backward_kernel, grid=(tiles,), in_specs=[pl.BlockSpec((2,...  13.6 us

profile of v3, /device:TPU:0, one launch (start us, length us, event | category | flops | bytes accessed | tf_op | source)
XLA Modules:
  0.0 85.5 jit_solution(9463191293952235749)
XLA Ops:
  0.0 71.8 %forward.1 = (bf16[2,4,2048,256]{3,2,1,0:T(8,128)(2,1)}, bf16[2,4,1024,256]{3,2,1,0:T(8,128)(2,1)}) custom-call(bf16[128,2048]{1,0:T(8,128)(2,1)} %basis_ref.1, s32[1,2048]{1,0:T(1,128)} %bitcast.5, f32[2,4,1,256]{3,2,1,0:T(1,128)} %bitcast.3, f32[16,1,128]{2,1,0:T(1,128)} %bitcast.4, bf16[2,2,256,2048]{3,2,1,0:T(8,128)(2,1)} %residual_ref.1), custom_call_target="tpu_custom_call" | custom-call | tf_op jit(solution)/shard_map/forward/pallas_call | solution.py:605
  71.8 13.6 %backward.1 = f32[2,2,256,2048]{3,2,1,0:T(8,128)} custom-call(bf16[2,4,1024,256]{3,2,1,0:T(8,128)(2,1)} %get-tuple-element.7.back_ref, bf16[2,4,2048,256]{3,2,1,0:T(8,128)(2,1)} %get-tuple-element.8.moved_ref), custom_call_target="tpu_custom_call" | custom-call | tf_op jit(solution)/shard_map/backward/pallas_call | solution.py:642

commit v4 on v3

--- a/solution.py
+++ b/solution.py
@@ -509,45 +509,44 @@
     def job(n, carry):
         b, last = block_at(n), block_at(n - 1)
 
-        @pl.when(n < BLOCKS)
+        @pl.when(n == 1)
         def _():
-            @pl.when(n == 1)
+            lax.fori_loop(1, chips, from_y, 0)
+
+        permute(b)
+        store_moved(core, b).start()
+        after(n, 0)
+
+        def side(q, carry):
+            h = core + q * (1 - 2 * core)
+
+            @pl.when(q == 1)
             def _():
-                lax.fori_loop(1, chips, from_y, 0)
-
-            permute(b)
-            store_moved(core, b).start()
-            after(n, 0)
+                for t in range(2):
+                    hand_over(b, other, t).wait_recv()
+                store_moved(other, b).start()
+
+            to_modes(h, b)
+            pl.when(q == 1)(lambda: each_slab(b, lambda e: send_devs(e).start()))
+            after(n, 1 + q)
+            return carry
+
+        lax.fori_loop(0, 2, side, 0)
 
         @pl.when(n > 0)
         def _():
             settle(last)
 
-        @pl.when(n < BLOCKS)
-        def _():
-            def side(q, carry):
-                h = core + q * (1 - 2 * core)
-
-                @pl.when(q == 1)
-                def _():
-                    for t in range(2):
-                        hand_over(b, other, t).wait_recv()
-                    store_moved(other, b).start()
-
-                to_modes(h, b)
-                pl.when(q == 1)(lambda: each_slab(b, lambda e: send_devs(e).start()))
-                after(n, 1 + q)
-                return carry
-
-            lax.fori_loop(0, 2, side, 0)
-
-        @pl.when(n > 0)
-        def _():
-            finish(last)
-
         return carry
 
-    lax.fori_loop(0, BLOCKS + 1, job, 0)
+    lax.fori_loop(0, BLOCKS, job, 0)
+
+    def tail(m, carry):
+        pl.when(m == 2)(lambda: settle(block_at(BLOCKS - 1)))
+        finish(block_at(m))
+        return carry
+
+    lax.fori_loop(0, BLOCKS, tail, 0)
 
     others(owners, lambda e: send_devs(e).wait_send())
     if_owner(lambda: others(parts, lambda d: send_edges(d).wait_send()))

time: 85.7 us -> 81.3 us (0.949)
  Pallas kernels: 85.5 us -> 81.1 us
    pallas_call x1, Pallas kernels: 71.8 us -> 67.4 us  [on_device(): pl.pallas_call(functools.partial(forward_kernel, chips), out_shape=[jax.S...]
where the time goes in v4:
time: 81.3 us; the launch traced here: 81.1 us
  Pallas kernels  81.1 us (100%)
    pallas_call x1, Pallas kernels, on_device(): pl.pallas_call(functools.partial(forward_kernel, chips), out_shape=[jax.S...  67.4 us
    pallas_call x1, Pallas kernels, on_device(): pl.pallas_call(backward_kernel, grid=(tiles,), in_specs=[pl.BlockSpec((2,...  13.6 us

profile of v4, /device:TPU:0, one launch (start us, length us, event | category | flops | bytes accessed | tf_op | source)
XLA Modules:
  0.0 81.1 jit_solution(16255388508820394963)
XLA Ops:
  0.0 67.4 %forward.1 = (bf16[2,4,2048,256]{3,2,1,0:T(8,128)(2,1)}, bf16[2,4,1024,256]{3,2,1,0:T(8,128)(2,1)}) custom-call(bf16[128,2048]{1,0:T(8,128)(2,1)} %basis_ref.1, s32[1,2048]{1,0:T(1,128)} %bitcast.5, f32[2,4,1,256]{3,2,1,0:T(1,128)} %bitcast.3, f32[16,1,128]{2,1,0:T(1,128)} %bitcast.4, bf16[2,2,256,2048]{3,2,1,0:T(8,128)(2,1)} %residual_ref.1), custom_call_target="tpu_custom_call" | custom-call | tf_op jit(solution)/shard_map/forward/pallas_call | solution.py:604
  67.4 13.6 %backward.1 = f32[2,2,256,2048]{3,2,1,0:T(8,128)} custom-call(bf16[2,4,1024,256]{3,2,1,0:T(8,128)(2,1)} %get-tuple-element.7.back_ref, bf16[2,4,2048,256]{3,2,1,0:T(8,128)(2,1)} %get-tuple-element.8.moved_ref), custom_call_target="tpu_custom_call" | custom-call | tf_op jit(solution)/shard_map/backward/pallas_call | solution.py:641
